TPU v7x, 256 devices: a whole 4x4x8 slice. The times are simulated.
256 devices in a mesh: lat: 8 (over y, x_hi), lon: 32 (over x_lo, z, core).
Axes of the slice: x: 4 (x_hi: 2, x_lo: 2; x = x_hi * 2 + x_lo), y: 4, z: 8, core: 2. Of those that a mesh axis runs over, the one named last changes fastest.
Arguments:
- skip: bfloat16 [2, 192, 384, 512], P(None, 'lat', 'lon'), may hold values from -6 to 6
- coarse: bfloat16 [2, 48, 96, 2048], P(None, 'lat', 'lon'), may hold values from -6 to 6
- offsets: int32 [2], replicated, may hold values from 1 to 6, as said below
- bands: int32 [192], replicated, may hold values from 0 to 15, never falling along the last dimension, each value on 1 to 24 neighbouring positions
- qkv3_weight: bfloat16 [2048, 6144], P(None, 'lon')
- out3_weight: bfloat16 [2048, 2048], P('lon'), may hold values from -0.125 to 0.125
- up_weight: bfloat16 [2048, 512], replicated, may hold values from -0.125 to 0.125
- qkv1_weight: bfloat16 [512, 1536], replicated
- out1_weight: bfloat16 [512, 512], replicated, may hold values from -0.25 to 0.25
- mlp_in: bfloat16 [512, 2048], replicated, may hold values from -0.25 to 0.25
- mlp_out: bfloat16 [2048, 512], replicated, may hold values from -0.125 to 0.125
Outputs:
- refined: bfloat16 [2, 192, 384, 512], P(None, 'lat', 'lon')
Inputs may be any that keep to these rules, and one draw needn't show every extreme that they name: offsets[0] is the latitude shift and offsets[1] the longitude shift; one of the two equals 6. `bands`: band ids never fall along latitude; one band spans 1 to 24 rows.
All inputs are finite; a program needn't handle non-finite values.
Results may differ from a plain program's by a relative error of at most 0.02.
Values may be sent and summed in bfloat16 or wider, within the bound.
A program may use at most 128 MiB of HBM per device.

v0:
```python
import jax
import jax.numpy as jnp
from jax import lax
from jax.experimental import pallas as pl
from jax.experimental.pallas import tpu as pltpu
from jax.sharding import PartitionSpec as P

LATS = 8
LONS = 32
ROWS = 192
D3 = 2048
D1 = 512
FF = 2048
HEAD = 64
CELLS3 = 36
SCALE = HEAD**-0.5
EPS = 1e-05
HALF = 80
WIN = 2 * HALF
MASKED = -1e30

F32 = jnp.float32
BF = jnp.bfloat16
MESH = pl.DeviceIdType.MESH
ANY = pl.ANY


def dot(a, b):
    return jnp.dot(a, b, preferred_element_type=F32)


def dot_nt(a, b):
    return lax.dot_general(a, b, (((1,), (1,)), ((), ())), preferred_element_type=F32)


def normalize(values):
    centred = values - jnp.mean(values, axis=-1, keepdims=True)
    spread = jnp.mean(centred * centred, axis=-1, keepdims=True)
    return centred * lax.rsqrt(spread + EPS)


def column(n):
    return lax.broadcasted_iota(jnp.int32, (n, 1), 0)


def onehot(target, width):
    n = target.shape[0]
    hit = lax.broadcasted_iota(jnp.int32, (n, width), 1) == target
    return jnp.where(hit, 1.0, 0.0).astype(BF)


def frame_cell(n):
    half = (n >= HALF).astype(jnp.int32)
    m = n - HALF * half
    valid = m < 72
    level = (m >= 36).astype(jnp.int32)
    m = m - 36 * level
    row = (m * 43) >> 8
    return valid, level, row, m - 6 * row + 6 * half


def softmax_mix(q, k, v, bias):
    scores = dot_nt(q, k) * SCALE
    if bias is not None:
        scores = scores + bias
    weights = jnp.exp(scores - jnp.max(scores, axis=1, keepdims=True))
    total = jnp.sum(weights, axis=1, keepdims=True)
    return dot(weights.astype(BF), v) * (1.0 / total)


def kernel(
    offs,
    bands,
    coarse,
    skip,
    wq,
    wo,
    up,
    w1,
    wo1,
    wi,
    wf,
    out,
    xs,
    G,
    Wb,
    wov,
    upv,
    W4,
    cup,
    skv,
    Sp,
    E,
    skF,
    bias,
    Pl,
    Po,
    Xt,
    PK,
    msg,
    R,
    LE,
    w1v,
    wo1v,
    wiv,
    wfv,
    pk1,
    mix,
    Z,
    loc,
    own_send,
    ring_send,
    ring_recv,
    wx_send,
    wx_recv,
    ws_send,
    ws_recv,
    wr_send,
    wr_recv,
    w4_send,
    w4_recv,
    sk_send,
    sk_recv,
    aa_send,
    aa_recv,
    li_send,
    li_recv,
    lo_send,
    lo_recv,
    la_send,
    la_recv,
):
    lat = lax.axis_index("lat")
    lon = lax.axis_index("lon")
    xl = lon // 16
    z = lax.rem(lon // 2, 8)
    c = lax.rem(lon, 2)
    base = xl * 16

    def at(lat_, lon_):
        return {"lat": lat_, "lon": lon_}

    def chip(z_, c_):
        return at(lat, base + 2 * lax.rem(z_ + 8, 8) + c_)

    sibling = at(lat, lon + 1 - 2 * c)
    across = lax.rem(lon + 16, 32)
    near = at(lat, across)
    far = at(lat + 1 - 2 * lax.rem(lat, 2), across)
    lon_next = lax.rem(lon + 1, LONS)
    lon_prev = lax.rem(lon + LONS - 1, LONS)
    lat_next = lax.rem(lat + 1, LATS)
    lat_prev = lax.rem(lat + LATS - 1, LATS)

    def remote(src, dst, send, recv, device):
        return pltpu.make_async_remote_copy(
            src_ref=src, dst_ref=dst, send_sem=send, recv_sem=recv, device_id=device, device_id_type=MESH
        )

    loads = [
        pltpu.make_async_copy(src, dst, loc.at[i])
        for i, (src, dst) in enumerate(
            [(up, upv), (wo, wov), (wq, Wb.at[0]), (skip, skv), (w1, w1v), (wo1, wo1v), (wi, wiv), (wf, wfv)]
        )
    ]
    for load in loads:
        load.start()

    barrier = pltpu.get_barrier_semaphore()
    greeted = [chip(z + d, c_) for d in range(1, 8) for c_ in (0, 1)] + [
        sibling,
        near,
        far,
        at(lat, lon_next),
        at(lat, lon_prev),
        at(lat_next, lon),
        at(lat_prev, lon),
        at(lat_next, lon_next),
        at(lat_prev, lon_prev),
    ]
    for device in greeted:
        pl.semaphore_signal(barrier, inc=1, device_id=device, device_id_type=MESH)

    normed3 = normalize(coarse[...].astype(F32)).astype(BF)
    rest = jnp.zeros((16, 512), F32)
    i16 = column(16)
    for f in range(4):
        part = normed3[:, 512 * f : 512 * f + 512]
        xs[32 * f : 32 * f + 32, :] = part[0:32]
        pick = onehot(jnp.where((i16 >> 2) == f, i16 & 3, -1), 16)
        rest = rest + dot(pick, part[32:48])
    xs[128:144, :] = rest.astype(BF)

    pl.semaphore_wait(barrier, len(greeted))

    target = z // 4
    mine = lax.rem(z, 4) * 2 + c
    is_home = target == c
    own = [
        remote(xs, G.at[mine], own_send.at[0], ring_recv.at[mine], chip(z + 1, target)),
        remote(xs, G.at[mine], own_send.at[1], ring_recv.at[mine], chip(z - 1, target)),
    ]
    own_sib = remote(xs, G.at[mine], own_send.at[2], ring_recv.at[mine], sibling)
    for copy in own:
        copy.start()

    @pl.when(jnp.logical_not(is_home))
    def _():
        own_sib.start()

    def rows(j):
        return pl.ds(512 * j, 512)

    wx = [
        remote(wq.at[rows(j)], Wb.at[2, rows(j)], wx_send.at[j], wx_recv.at[j], near if j < 2 else far)
        for j in (0, 2, 1, 3)
    ]
    for copy in wx:
        copy.start()
    ws = remote(wq, Wb.at[1], ws_send.at[0], ws_recv.at[0], sibling)
    ws.start()

    loads[0].wait()
    loads[1].wait()
    W4[0:64, :] = dot(wov[...], upv[...]).astype(BF)
    w4x = remote(W4.at[0:64], W4.at[128:192], w4_send.at[0], w4_recv.at[0], near)
    w4x.start()
    w4s = remote(W4.at[0:64], W4.at[64:128], w4_send.at[1], w4_recv.at[1], sibling)
    w4s.start()
    cup[...] = dot(coarse[...], upv[...])

    @pl.when(is_home)
    def _():
        G[pl.ds(mine, 1)] = xs[...].reshape(1, 144, 512)

    def relay(k, way):
        return remote(
            G.at[k], G.at[k], ring_send.at[k, way], ring_recv.at[k], chip(z + (1 if way == 0 else -1), c)
        )

    def ring_steps(s):
        for way in (0, 1):
            source = lax.rem(z + (8 - s if way == 0 else s), 8)
            for core in (0, 1):
                limit = 4 if core == way else 3
                if s <= limit:
                    yield way, lax.rem(source, 4) * 2 + core, source // 4 == c, s < limit

    def ring(s):
        for way, k, here, onward in ring_steps(s):

            @pl.when(here)
            def _(way=way, k=k, onward=onward):
                copy = relay(k, way)
                copy.wait_recv()
                if onward:
                    copy.start()

    ring(1)

    loads[3].wait()
    Sp[...] = jnp.zeros_like(Sp)
    for k in range(48):
        Sp[16 * k : 16 * k + 12, :] = skv[k]
    r192 = column(192)
    spread = onehot(((r192 >> 3) & 1) * 128 + (r192 & 7) * 16 + (r192 >> 4), 256)
    for b in range(3):
        E[b, 0:192, :] = (
            dot(spread[:, 0:128], Sp[128 * b : 128 * b + 128, :])
            + dot(spread[:, 128:256], Sp[384 + 128 * b : 384 + 128 * b + 128, :])
        ).astype(BF)

    ring(2)

    a = offs[0]
    shift_lat = jnp.where(a >= 6, a - 6, a)
    shift_lon = offs[1]
    n = column(WIN)
    valid, level, row, col = frame_cell(n)
    valid_t, _, row_t, _ = frame_cell(lax.broadcasted_iota(jnp.int32, (1, WIN), 1))
    source_col = col + shift_lon
    for w in range(4):
        source_row = row + (shift_lat + 6 * w)
        over = (source_row >= 24).astype(jnp.int32)
        coarse_row = source_row >> 2
        coarse_col = source_col >> 2
        row_out = (coarse_row >= 6).astype(jnp.int32)
        col_out = (coarse_col >= 3).astype(jnp.int32)
        cell = 48 * (col_out + 2 * row_out) + 18 * level + 3 * (coarse_row - 6 * row_out) + coarse_col - 3 * col_out
        Pl[w] = onehot(jnp.where(valid, cell, -1), 192)
        label = jnp.zeros((WIN, 1), jnp.int32)
        label_t = jnp.zeros((1, WIN), jnp.int32)
        for i in range(6):
            band = bands[lax.rem(lat * 24 + shift_lat + (6 * w + i), ROWS)]
            label = jnp.where(row == i, band, label)
            label_t = jnp.where(row_t == i, band, label_t)
        free = jnp.where(valid, 0, 1)
        seen = jnp.where(valid_t, 1, 0)
        match = jnp.where(label == label_t, 1, 0)
        bias[w] = jnp.where(seen * (match + free) > 0, 0.0, MASKED)

    r = column(192)
    out_level = (r >= 96).astype(jnp.int32)
    out_col = r & 15
    frame_row = ((r - 96 * out_level) >> 4) - shift_lat
    before = (frame_row < 0).astype(jnp.int32)
    inner = 36 * out_level + 6 * (frame_row + 6 * before)
    frame_col = out_col - shift_lon
    left = frame_col < 0
    second = (frame_col >= 6).astype(jnp.int32)
    place = jnp.where(left, 160 + 6 + frame_col, HALF * second + frame_col - 6 * second)
    Po[...] = onehot(jnp.where(out_col < 12, 240 * (1 - before) + inner + place, -1), 480)

    ring(3)

    sk = [
        remote(E.at[0:3, 0:96], E.at[0:3, 192:288], sk_send.at[0], sk_recv.at[0], at(lat, lon_prev)),
        remote(E.at[0, 0:192], E.at[3, 0:192], sk_send.at[1], sk_recv.at[1], at(lat_prev, lon)),
        remote(E.at[0, 0:96], E.at[3, 192:288], sk_send.at[2], sk_recv.at[2], at(lat_prev, lon_prev)),
    ]
    for copy in sk:
        copy.start()

    w4x.wait_recv()
    w4r = remote(W4.at[128:192], W4.at[192:256], w4_send.at[2], w4_recv.at[2], sibling)
    w4r.start()
    wr = [
        remote(Wb.at[2, rows(j)], Wb.at[3, rows(j)], wr_send.at[j], wr_recv.at[j], sibling) for j in (0, 2, 1, 3)
    ]
    for arrived, onward in zip(wx, wr):
        arrived.wait_recv()
        onward.start()

    ring(4)

    @pl.when(is_home)
    def _():
        k = lax.rem(z, 4) * 2 + (1 - c)
        remote(xs, G.at[k], own_send.at[2], ring_recv.at[k], sibling).wait_recv()

    for w in range(2):
        tails = G[4 * w : 4 * w + 4, 128:144, :].reshape(64, 512)
        for f in range(4):
            pick = onehot((i16 >> 2) * 16 + 4 * f + (i16 & 3), 64)
            Xt[16 * w : 16 * w + 16, 512 * f : 512 * f + 512] = dot(pick, tails).astype(BF)

    loads[2].wait()
    ws.wait_recv()
    for copy in wr:
        copy.wait_recv()
    w4s.wait_recv()
    w4r.wait_recv()

    for h in range(4):
        main = jnp.zeros((256, 192), F32)
        for f in range(4):
            main = main + dot(
                G[:, 32 * f : 32 * f + 32, :].reshape(256, 512), Wb[h, 512 * f : 512 * f + 512, :]
            )
        tail = dot(Xt[...], Wb[h])
        for w in range(2):
            PK[h, w, 0:128, :] = main[128 * w : 128 * w + 128].astype(BF)
            PK[h, w, 128:144, :] = tail[16 * w : 16 * w + 16].astype(BF)

    i64 = column(64)
    for w in range(2):
        terms = jnp.zeros((144, 512), F32)
        for h in range(4):
            packed = PK[h, w]
            mixed = softmax_mix(packed[:, 0:64], packed[:, 64:128], packed[:, 128:192], None).astype(BF)
            terms = terms + dot(mixed, W4[64 * h : 64 * h + 64, :])
        terms = terms.astype(BF)
        tails = jnp.zeros((64, 128), F32)
        for f in range(4):
            part = terms[:, 128 * f : 128 * f + 128]
            for q in range(4):
                msg[4 * w + q, 32 * f : 32 * f + 32, :] = part[32 * q : 32 * q + 32]
            tails = tails + dot(
                onehot(jnp.where(((i64 >> 2) & 3) == f, (i64 >> 4) * 4 + (i64 & 3), -1), 16), part[128:144]
            )
        tails = tails.astype(BF)
        for q in range(4):
            msg[4 * w + q, 128:144, :] = tails[16 * q : 16 * q + 16]

    def term(k):
        return remote(msg.at[k], R.at[z], aa_send.at[k], aa_recv.at[z], at(lat, base + 8 * c + k))

    for k in range(8):

        @pl.when(base + 8 * c + k != lon)
        def _(k=k):
            term(k).start()

    @pl.when(is_home)
    def _():
        R[pl.ds(z, 1)] = msg[pl.ds(mine, 1)]

    total = jnp.zeros((144, 128), F32)
    for s in range(8):

        @pl.when(base + 2 * s + target != lon)
        def _(s=s):
            remote(msg.at[0], R.at[s], aa_send.at[0], aa_recv.at[s], sibling).wait_recv()

    for s in range(8):
        total = total + R[s].astype(F32)
    for f in range(4):
        lanes = slice(128 * f, 128 * f + 128)
        LE[0:32, lanes] = (cup[0:32, lanes] + total[32 * f : 32 * f + 32]).astype(BF)
        pick = jnp.where(
            (lax.broadcasted_iota(jnp.int32, (16, 16), 1) == 4 * f + i16) & (i16 < 4), 1.0, 0.0
        )
        rest = jnp.dot(pick, total[128:144], preferred_element_type=F32, precision=lax.Precision.HIGHEST)
        LE[32:48, lanes] = (cup[32:48, lanes] + rest).astype(BF)

    li = [
        remote(LE.at[0:48], LE.at[48:96], li_send.at[0], li_recv.at[0], at(lat, lon_prev)),
        remote(LE.at[0:48], LE.at[96:144], li_send.at[1], li_recv.at[1], at(lat_prev, lon)),
        remote(LE.at[0:48], LE.at[144:192], li_send.at[2], li_recv.at[2], at(lat_prev, lon_prev)),
    ]
    for copy in li:
        copy.start()

    for copy in sk:
        copy.wait_recv()
    for w in range(4):
        source_row = row + (shift_lat + 6 * w)
        first = w // 2
        cell = 288 * ((source_row >> 3) - first) + 16 * source_col + 8 * level + (source_row & 7)
        cell = jnp.where(valid, cell, -1)
        taken = jnp.zeros((WIN, D1), F32)
        for b in range(3):
            taken = taken + dot(onehot(cell - 288 * b, 288), E[first + b])
        skF[w] = taken.astype(BF)

    for load in loads[4:]:
        load.wait()
    for copy in li:
        copy.wait_recv()

    def window(t, carry):
        w = lax.rem(t + 3, 4)
        stream = skF[w].astype(F32) + dot(Pl[w], LE[...])
        pk1[...] = dot(normalize(stream).astype(BF), w1v[...]).astype(BF)
        allowed = bias[w]
        for pair in range(4):
            both = []
            for h in (2 * pair, 2 * pair + 1):
                q = pk1[:, 192 * h : 192 * h + 64]
                k = pk1[:, 192 * h + 64 : 192 * h + 128]
                v = pk1[:, 192 * h + 128 : 192 * h + 192]
                both.append(softmax_mix(q, k, v, allowed))
            mix[:, 128 * pair : 128 * pair + 128] = jnp.concatenate(both, axis=1).astype(BF)
        attended = stream + dot(mix[...], wo1v[...])
        normed2 = normalize(attended).astype(BF)
        result = attended
        for f in range(2):
            hidden = jax.nn.gelu(dot(normed2, wiv[:, 1024 * f : 1024 * f + 1024])).astype(BF)
            result = result + dot(hidden, wfv[1024 * f : 1024 * f + 1024, :])
        Z[w + 1, 0:WIN, :] = result.astype(BF)
        to_lon(w).start()

        @pl.when(t == 0)
        def _():
            to_lat.start()
            to_both.start()

        return carry

    def to_lon(w):
        return remote(
            Z.at[w + 1, HALF:WIN], Z.at[w + 1, WIN : WIN + HALF], lo_send.at[w], lo_recv.at[w], at(lat, lon_next)
        )

    to_lat = remote(Z.at[4, 0:WIN], Z.at[0, 0:WIN], la_send.at[0], la_recv.at[0], at(lat_next, lon))
    to_both = remote(
        Z.at[4, HALF:WIN], Z.at[0, WIN : WIN + HALF], la_send.at[1], la_recv.at[1], at(lat_next, lon_next)
    )
    lax.fori_loop(0, 4, window, 0)

    to_lat.wait_recv()
    to_both.wait_recv()
    for w in (3, 0, 1, 2):
        to_lon(w).wait_recv()
    for v in range(4):
        taken = dot(Po[:, 0:240], Z[v]) + dot(Po[:, 240:480], Z[v + 1])
        taken = taken.astype(BF)
        out[96 * v : 96 * v + 96, :] = taken[0:96]
        out[384 + 96 * v : 384 + 96 * v + 96, :] = taken[96:192]

    for copy in [*own, *wx, ws, w4x, w4s, w4r, *wr, *sk, *li, to_lat, to_both]:
        copy.wait_send()

    @pl.when(jnp.logical_not(is_home))
    def _():
        own_sib.wait_send()

    for s in (1, 2, 3):
        for way, k, here, onward in ring_steps(s):
            if onward:

                @pl.when(here)
                def _(way=way, k=k):
                    relay(k, way).wait_send()

    for k in range(8):

        @pl.when(base + 8 * c + k != lon)
        def _(k=k):
            term(k).wait_send()

    for w in range(4):
        to_lon(w).wait_send()


def local(
    skip,
    coarse,
    offsets,
    bands,
    qkv3_weight,
    out3_weight,
    up_weight,
    qkv1_weight,
    out1_weight,
    mlp_in,
    mlp_out,
):
    cells = jnp.pad(coarse.reshape(CELLS3, D3), ((0, 12), (0, 0)))
    vmem = pl.BlockSpec(memory_space=pltpu.VMEM)
    smem = pl.BlockSpec(memory_space=pltpu.SMEM)
    hbm = pl.BlockSpec(memory_space=ANY)
    dma = pltpu.SemaphoreType.DMA
    placed = pl.pallas_call(
        kernel,
        out_shape=jax.ShapeDtypeStruct((768, D1), BF),
        in_specs=[smem, smem, vmem] + [hbm] * 8,
        out_specs=vmem,
        scratch_shapes=[
            pltpu.VMEM((144, 512), BF),
            pltpu.VMEM((8, 144, 512), BF),
            pltpu.VMEM((4, D3, 192), BF),
            pltpu.VMEM((64, D3), BF),
            pltpu.VMEM((D3, D1), BF),
            pltpu.VMEM((256, D1), BF),
            pltpu.VMEM((48, D1), F32),
            pltpu.VMEM((48, 12, D1), BF),
            pltpu.VMEM((768, D1), BF),
            pltpu.VMEM((4, 288, D1), BF),
            pltpu.VMEM((4, WIN, D1), BF),
            pltpu.VMEM((4, WIN, WIN), F32),
            pltpu.VMEM((4, WIN, 192), BF),
            pltpu.VMEM((192, 480), BF),
            pltpu.VMEM((32, D3), BF),
            pltpu.VMEM((4, 2, 144, 192), BF),
            pltpu.VMEM((8, 144, 128), BF),
            pltpu.VMEM((8, 144, 128), BF),
            pltpu.VMEM((192, D1), BF),
            pltpu.VMEM((D1, 3 * D1), BF),
            pltpu.VMEM((D1, D1), BF),
            pltpu.VMEM((D1, FF), BF),
            pltpu.VMEM((FF, D1), BF),
            pltpu.VMEM((WIN, 3 * D1), BF),
            pltpu.VMEM((WIN, D1), BF),
            pltpu.VMEM((5, 240, D1), BF),
            dma((8,)),
            dma((3,)),
            dma((8, 2)),
            dma((8,)),
            dma((4,)),
            dma((4,)),
            dma((1,)),
            dma((1,)),
            dma((4,)),
            dma((4,)),
            dma((3,)),
            dma((3,)),
            dma((3,)),
            dma((3,)),
            dma((8,)),
            dma((8,)),
            dma((3,)),
            dma((3,)),
            dma((4,)),
            dma((4,)),
            dma((2,)),
            dma((2,)),
        ],
        compiler_params=pltpu.CompilerParams(
            collective_id=0, has_side_effects=True, vmem_limit_bytes=56 * 1024 * 1024
        ),
    )(
        offsets,
        bands,
        cells,
        skip.reshape(48, 12, D1),
        qkv3_weight,
        out3_weight,
        up_weight,
        qkv1_weight,
        out1_weight,
        mlp_in,
        mlp_out,
    )
    return placed.reshape(2, 24, 16, D1)[:, :, :12]


def solution(mesh):
    return jax.shard_map(
        local,
        mesh=mesh,
        in_specs=(
            P(None, "lat", "lon", None),
            P(None, "lat", "lon", None),
            P(),
            P(),
            P(None, "lon"),
            P("lon", None),
            P(),
            P(),
            P(),
            P(),
            P(),
        ),
        out_specs=P(None, "lat", "lon", None),
        check_vma=False,
    )
```

profile of v0, /device:TPU:30, one launch (start us, length us, event | category | flops | bytes accessed | tf_op | source)
XLA Modules:
  0.0 73.4 jit_solution(16031982374459261748)
XLA Ops:
  0.0 0.0 copy-start
  0.0 1.1 %copy.16 = bf16[2,6,3,2048]{3,2,1,0:T(4,128)(2,1)S(1)} copy(bf16[2,6,3,2048]{3,0,2,1:T(2,128)(2,1)} %param.12) | data formatting | bytes 294912 | tf_op args[1]
  1.1 0.1 reshape.9
  1.2 0.7 pad.4.coarse
  1.9 2.2 %copy.17 = bf16[2,24,12,512]{3,2,1,0:T(8,128)(2,1)} copy(bf16[2,24,12,512]{3,1,2,0:T(8,128)(2,1)} %param.11) | data formatting | bytes 1179648 | tf_op args[0]
  4.1 0.0 copy-done
  4.1 1.3 %copy.18.wq = bf16[2048,192]{1,0:T(8,128)(2,1)} copy(bf16[2048,192]{0,1:T(8,128)(2,1)S(1)} %copy-done) | data formatting | bytes 1572864 | tf_op args[4]
  5.4 65.7 %shard_map.109 = bf16[768,512]{1,0:T(8,128)(2,1)} custom-call(s32[2]{0:T(128)} %offs.1, s32[192]{0:T(256)} %bands.1, bf16[48,2048]{1,0:T(8,128)(2,1)} %pad.4.coarse, bf16[48,12,512]{2,1,0:T(8,128)(2,1)} %bitcast.4, bf16[2048,192]{1,0:T(8,128)(2,1)} %copy.18.wq, bf16[64,2048]{1,0:T(8,128)(2,1)} %wo.1, bf16[2048,512]{1,0:T(8,128)(2,1)} %up.1, ...), custom_call_target="tpu_custom_call" | custom-call | tf_op jit(solution)/shard_map/pallas_call | solution.py:534
  71.1 2.3 %copy.20 = bf16[2,24,12,512]{3,1,2,0:T(8,128)(2,1)} copy(bf16[2,24,12,512]{3,2,1,0:T(8,128)(2,1)} %bitcast.3) | data formatting | bytes 1179648
Async XLA Ops:
  0.0 4.1 %copy-start = (bf16[2048,192]{0,1:T(8,128)(2,1)S(1)}, bf16[2048,192]{0,1:T(8,128)(2,1)}, u32[]{:S(2)}) copy-start(bf16[2048,192]{0,1:T(8,128)(2,1)} %param.15) | copy-start | bytes 2359300
where the time goes:
time: 74.3 us; the launch traced here: 73.4 us
  Pallas kernels  65.7 us (88%)
  local copies, waits for them, and re-layouts  7.67 us (10%)
    pallas_call x1, Pallas kernels, local(): pl.pallas_call(kernel, out_shape=jax.ShapeDtypeStruct((768, D1), BF), in_...  65.7 us
    unnamed x6, local copies, waits for them, and re-layouts  6.85 us

commit v1 on v0

--- a/solution.py
+++ b/solution.py
@@ -13,6 +13,7 @@
 FF = 2048
 HEAD = 64
 CELLS3 = 36
+OWN = 576
 SCALE = HEAD**-0.5
 EPS = 1e-05
 HALF = 80
@@ -88,7 +89,6 @@
     upv,
     W4,
     cup,
-    skv,
     Sp,
     E,
     skF,
@@ -160,7 +160,7 @@
     loads = [
         pltpu.make_async_copy(src, dst, loc.at[i])
         for i, (src, dst) in enumerate(
-            [(up, upv), (wo, wov), (wq, Wb.at[0]), (skip, skv), (w1, w1v), (wo1, wo1v), (wi, wiv), (wf, wfv)]
+            [(up, upv), (wo, wov), (wq, Wb.at[0]), (skip, E.at[0:OWN]), (w1, w1v), (wo1, wo1v), (wi, wiv), (wf, wfv)]
         )
     ]
     for load in loads:
@@ -181,7 +181,10 @@
     for device in greeted:
         pl.semaphore_signal(barrier, inc=1, device_id=device, device_id_type=MESH)
 
-    normed3 = normalize(coarse[...].astype(F32)).astype(BF)
+    cells = coarse[...].astype(F32).reshape(CELLS3, D3)
+    cells = jnp.concatenate([cells, jnp.zeros((12, D3), F32)], axis=0)
+    normed3 = normalize(cells).astype(BF)
+    cells = cells.astype(BF)
     rest = jnp.zeros((16, 512), F32)
     i16 = column(16)
     for f in range(4):
@@ -209,7 +212,7 @@
         own_sib.start()
 
     def rows(j):
-        return pl.ds(512 * j, 512)
+        return pl.ds(48 * j, 48)
 
     wx = [
         remote(wq.at[rows(j)], Wb.at[2, rows(j)], wx_send.at[j], wx_recv.at[j], near if j < 2 else far)
@@ -227,7 +230,7 @@
     w4x.start()
     w4s = remote(W4.at[0:64], W4.at[64:128], w4_send.at[1], w4_recv.at[1], sibling)
     w4s.start()
-    cup[...] = dot(coarse[...], upv[...])
+    cup[...] = dot(cells, upv[...])
 
     @pl.when(is_home)
     def _():
@@ -259,16 +262,9 @@
     ring(1)
 
     loads[3].wait()
-    Sp[...] = jnp.zeros_like(Sp)
-    for k in range(48):
-        Sp[16 * k : 16 * k + 12, :] = skv[k]
     r192 = column(192)
-    spread = onehot(((r192 >> 3) & 1) * 128 + (r192 & 7) * 16 + (r192 >> 4), 256)
-    for b in range(3):
-        E[b, 0:192, :] = (
-            dot(spread[:, 0:128], Sp[128 * b : 128 * b + 128, :])
-            + dot(spread[:, 128:256], Sp[384 + 128 * b : 384 + 128 * b + 128, :])
-        ).astype(BF)
+    first_rows = onehot(((r192 >> 3) & 1) * 288 + (r192 >> 4) * 24 + (r192 & 7), OWN)
+    Sp[...] = dot(first_rows, E[0:OWN, :]).astype(BF)
 
     ring(2)
 
@@ -281,12 +277,11 @@
     source_col = col + shift_lon
     for w in range(4):
         source_row = row + (shift_lat + 6 * w)
-        over = (source_row >= 24).astype(jnp.int32)
         coarse_row = source_row >> 2
         coarse_col = source_col >> 2
         row_out = (coarse_row >= 6).astype(jnp.int32)
         col_out = (coarse_col >= 3).astype(jnp.int32)
-        cell = 48 * (col_out + 2 * row_out) + 18 * level + 3 * (coarse_row - 6 * row_out) + coarse_col - 3 * col_out
+        cell = 48 * (col_out + 2 * row_out) + level + 6 * (coarse_row - 6 * row_out) + 2 * (coarse_col - 3 * col_out)
         Pl[w] = onehot(jnp.where(valid, cell, -1), 192)
         label = jnp.zeros((WIN, 1), jnp.int32)
         label_t = jnp.zeros((1, WIN), jnp.int32)
@@ -301,22 +296,23 @@
 
     r = column(192)
     out_level = (r >= 96).astype(jnp.int32)
-    out_col = r & 15
-    frame_row = ((r - 96 * out_level) >> 4) - shift_lat
-    before = (frame_row < 0).astype(jnp.int32)
-    inner = 36 * out_level + 6 * (frame_row + 6 * before)
-    frame_col = out_col - shift_lon
+    frame_col = ((r - 96 * out_level) >> 3) - shift_lon
     left = frame_col < 0
     second = (frame_col >= 6).astype(jnp.int32)
     place = jnp.where(left, 160 + 6 + frame_col, HALF * second + frame_col - 6 * second)
-    Po[...] = onehot(jnp.where(out_col < 12, 240 * (1 - before) + inner + place, -1), 480)
+    for b in range(3):
+        frame_row = (r & 7) + (8 * b + 6) - shift_lat
+        slot = (frame_row * 43) >> 8
+        inner = 36 * out_level + 6 * (frame_row - 6 * slot)
+        Po[b] = onehot(240 * (slot - b) + inner + place, 720)
 
     ring(3)
 
     sk = [
-        remote(E.at[0:3, 0:96], E.at[0:3, 192:288], sk_send.at[0], sk_recv.at[0], at(lat, lon_prev)),
-        remote(E.at[0, 0:192], E.at[3, 0:192], sk_send.at[1], sk_recv.at[1], at(lat_prev, lon)),
-        remote(E.at[0, 0:96], E.at[3, 192:288], sk_send.at[2], sk_recv.at[2], at(lat_prev, lon_prev)),
+        remote(E.at[0:144], E.at[576:720], sk_send.at[0], sk_recv.at[0], at(lat, lon_prev)),
+        remote(E.at[288:432], E.at[720:864], sk_send.at[1], sk_recv.at[1], at(lat, lon_prev)),
+        remote(Sp, E.at[864:1056], sk_send.at[2], sk_recv.at[2], at(lat_prev, lon)),
+        remote(Sp.at[0:96], E.at[1056:1152], sk_send.at[3], sk_recv.at[3], at(lat_prev, lon_prev)),
     ]
     for copy in sk:
         copy.start()
@@ -354,10 +350,10 @@
     for h in range(4):
         main = jnp.zeros((256, 192), F32)
         for f in range(4):
-            main = main + dot(
-                G[:, 32 * f : 32 * f + 32, :].reshape(256, 512), Wb[h, 512 * f : 512 * f + 512, :]
+            main = main + dot_nt(
+                G[:, 32 * f : 32 * f + 32, :].reshape(256, 512), Wb[h, :, 512 * f : 512 * f + 512]
             )
-        tail = dot(Xt[...], Wb[h])
+        tail = dot_nt(Xt[...], Wb[h])
         for w in range(2):
             PK[h, w, 0:128, :] = main[128 * w : 128 * w + 128].astype(BF)
             PK[h, w, 128:144, :] = tail[16 * w : 16 * w + 16].astype(BF)
@@ -425,13 +421,15 @@
         copy.wait_recv()
     for w in range(4):
         source_row = row + (shift_lat + 6 * w)
-        first = w // 2
-        cell = 288 * ((source_row >> 3) - first) + 16 * source_col + 8 * level + (source_row & 7)
-        cell = jnp.where(valid, cell, -1)
-        taken = jnp.zeros((WIN, D1), F32)
-        for b in range(3):
-            taken = taken + dot(onehot(cell - 288 * b, 288), E[first + b])
-        skF[w] = taken.astype(BF)
+        cell = jnp.where(
+            source_col < 12,
+            288 * level + 24 * source_col + source_row,
+            576 + 144 * level + 24 * (source_col - 12) + source_row,
+        )
+        below = 864 + 16 * source_col + 8 * level + source_row - 24
+        cell = jnp.where(source_row < 24, cell, below)
+        width = 1152 if w == 3 else 864
+        skF[w] = dot(onehot(jnp.where(valid, cell, -1), width), E[0:width, :]).astype(BF)
 
     for load in loads[4:]:
         load.wait()
@@ -482,11 +480,9 @@
     to_both.wait_recv()
     for w in (3, 0, 1, 2):
         to_lon(w).wait_recv()
-    for v in range(4):
-        taken = dot(Po[:, 0:240], Z[v]) + dot(Po[:, 240:480], Z[v + 1])
-        taken = taken.astype(BF)
-        out[96 * v : 96 * v + 96, :] = taken[0:96]
-        out[384 + 96 * v : 384 + 96 * v + 96, :] = taken[96:192]
+    for b in range(3):
+        taken = dot(Po[b, :, 0:240], Z[b]) + dot(Po[b, :, 240:480], Z[b + 1]) + dot(Po[b, :, 480:720], Z[b + 2])
+        out[:, 8 * b : 8 * b + 8, :] = taken.astype(BF).reshape(24, 8, D1)
 
     for copy in [*own, *wx, ws, w4x, w4s, w4r, *wr, *sk, *li, to_lat, to_both]:
         copy.wait_send()
@@ -526,31 +522,30 @@
     mlp_in,
     mlp_out,
 ):
-    cells = jnp.pad(coarse.reshape(CELLS3, D3), ((0, 12), (0, 0)))
+    cells = jnp.transpose(coarse, (1, 2, 0, 3)).reshape(CELLS3 // 2, 2, D3)
     vmem = pl.BlockSpec(memory_space=pltpu.VMEM)
     smem = pl.BlockSpec(memory_space=pltpu.SMEM)
     hbm = pl.BlockSpec(memory_space=ANY)
     dma = pltpu.SemaphoreType.DMA
     placed = pl.pallas_call(
         kernel,
-        out_shape=jax.ShapeDtypeStruct((768, D1), BF),
+        out_shape=jax.ShapeDtypeStruct((24, 24, D1), BF),
         in_specs=[smem, smem, vmem] + [hbm] * 8,
         out_specs=vmem,
         scratch_shapes=[
             pltpu.VMEM((144, 512), BF),
             pltpu.VMEM((8, 144, 512), BF),
-            pltpu.VMEM((4, D3, 192), BF),
+            pltpu.VMEM((4, 192, D3), BF),
             pltpu.VMEM((64, D3), BF),
             pltpu.VMEM((D3, D1), BF),
             pltpu.VMEM((256, D1), BF),
             pltpu.VMEM((48, D1), F32),
-            pltpu.VMEM((48, 12, D1), BF),
-            pltpu.VMEM((768, D1), BF),
-            pltpu.VMEM((4, 288, D1), BF),
+            pltpu.VMEM((192, D1), BF),
+            pltpu.VMEM((1152, D1), BF),
             pltpu.VMEM((4, WIN, D1), BF),
             pltpu.VMEM((4, WIN, WIN), F32),
             pltpu.VMEM((4, WIN, 192), BF),
-            pltpu.VMEM((192, 480), BF),
+            pltpu.VMEM((3, 192, 720), BF),
             pltpu.VMEM((32, D3), BF),
             pltpu.VMEM((4, 2, 144, 192), BF),
             pltpu.VMEM((8, 144, 128), BF),
@@ -575,8 +570,8 @@
             dma((4,)),
             dma((3,)),
             dma((3,)),
-            dma((3,)),
-            dma((3,)),
+            dma((4,)),
+            dma((4,)),
             dma((8,)),
             dma((8,)),
             dma((3,)),
@@ -593,8 +588,8 @@
         offsets,
         bands,
         cells,
-        skip.reshape(48, 12, D1),
-        qkv3_weight,
+        jnp.transpose(skip, (0, 2, 1, 3)).reshape(OWN, D1),
+        qkv3_weight.T,
         out3_weight,
         up_weight,
         qkv1_weight,
@@ -602,7 +597,7 @@
         mlp_in,
         mlp_out,
     )
-    return placed.reshape(2, 24, 16, D1)[:, :, :12]
+    return jnp.transpose(placed.reshape(2, 12, 24, D1), (0, 2, 1, 3))
 
 
 def solution(mesh):

time: 74.3 us -> 68.9 us (0.927)
  the two profiles are of different devices: /device:TPU:30 before, /device:TPU:80 now
where the time goes in v1:
time: 68.9 us; the launch traced here: 68.7 us
  Pallas kernels  66.8 us (97%)
  local copies, waits for them, and re-layouts  1.92 us (3%)
    pallas_call x1, Pallas kernels, local(): pl.pallas_call(kernel, out_shape=jax.ShapeDtypeStruct((24, 24, D1), BF),...  66.8 us
    unnamed x1, local copies, waits for them, and re-layouts  1.92 us

profile of v1, /device:TPU:80, one launch (start us, length us, event | category | flops | bytes accessed | tf_op | source)
XLA Modules:
  0.0 68.7 jit_solution(13072682426282083695)
XLA Ops:
  0.0 66.8 %shard_map.109 = bf16[24,24,512]{2,1,0:T(8,128)(2,1)} custom-call(s32[2]{0:T(128)} %offs.1, s32[192]{0:T(256)} %bands.1, bf16[18,2,2048]{2,1,0:T(2,128)(2,1)} %bitcast.13, bf16[576,512]{1,0:T(8,128)(2,1)} %bitcast.12, bf16[192,2048]{1,0:T(8,128)(2,1)} %bitcast.11, bf16[64,2048]{1,0:T(8,128)(2,1)} %wo.1, bf16[2048,512]{1,0:T(8,128)(2,1)} %up.1, ...), custom_call_target="tpu_custom_call" | custom-call | tf_op jit(solution)/shard_map/pallas_call | solution.py:530
  66.8 1.9 %copy.13 = bf16[2,24,12,512]{3,1,2,0:T(8,128)(2,1)} copy(bf16[2,24,12,512]{3,1,2,0:T(8,128)(2,1)} %bitcast.10) | data formatting | bytes 1179648

commit v2 on v1

--- a/solution.py
+++ b/solution.py
@@ -54,10 +54,8 @@
     half = (n >= HALF).astype(jnp.int32)
     m = n - HALF * half
     valid = m < 72
-    level = (m >= 36).astype(jnp.int32)
-    m = m - 36 * level
-    row = (m * 43) >> 8
-    return valid, level, row, m - 6 * row + 6 * half
+    sixth = (m * 43) >> 8
+    return valid, sixth & 1, 5 - (sixth >> 1), m - 6 * sixth + 6 * half
 
 
 def softmax_mix(q, k, v, bias):
@@ -194,6 +192,9 @@
         rest = rest + dot(pick, part[32:48])
     xs[128:144, :] = rest.astype(BF)
 
+    for first in (64, 144, 224):
+        Z[0, first : first + 16, :] = jnp.zeros((16, D1), BF)
+
     pl.semaphore_wait(barrier, len(greeted))
 
     target = z // 4
@@ -259,14 +260,18 @@
                 if onward:
                     copy.start()
 
+    loads[3].wait()
+    r128 = column(128)
+    r64 = r128 & 63
+    ten = (r64 * 103) >> 10
+    five = (r64 * 205) >> 10
+    first_rows = (five & 1) * 288 + (ten + 6 * (r128 >> 6)) * 24 + r64 - 5 * five
+    Sp[...] = dot(onehot(jnp.where(r64 < 60, first_rows, -1), OWN), E[0:OWN, :]).astype(BF)
+
+    sk_lat = remote(Sp, E.at[864:992], sk_send.at[2], sk_recv.at[2], at(lat_prev, lon))
+    sk_lat.start()
+
     ring(1)
-
-    loads[3].wait()
-    r192 = column(192)
-    first_rows = onehot(((r192 >> 3) & 1) * 288 + (r192 >> 4) * 24 + (r192 & 7), OWN)
-    Sp[...] = dot(first_rows, E[0:OWN, :]).astype(BF)
-
-    ring(2)
 
     a = offs[0]
     shift_lat = jnp.where(a >= 6, a - 6, a)
@@ -275,14 +280,47 @@
     valid, level, row, col = frame_cell(n)
     valid_t, _, row_t, _ = frame_cell(lax.broadcasted_iota(jnp.int32, (1, WIN), 1))
     source_col = col + shift_lon
+    r = column(192)
+    out_level = (r >= 96).astype(jnp.int32)
+    frame_col = ((r - 96 * out_level) >> 3) - shift_lon
+    left = frame_col < 0
+    second = (frame_col >= 6).astype(jnp.int32)
+    place = jnp.where(left, 160 + 6 + frame_col, HALF * second + frame_col - 6 * second)
+    for b in range(3):
+        frame_row = (r & 7) + (8 * b + 6) - shift_lat
+        slot = (frame_row * 43) >> 8
+        inner = 12 * (5 - (frame_row - 6 * slot)) + 6 * out_level
+        Po[b] = onehot(240 * (slot - b) + inner + place, 720)
+
+    ring(2)
+
+    ring(3)
+
+    sk_lon = [
+        remote(E.at[0:144], E.at[576:720], sk_send.at[0], sk_recv.at[0], at(lat, lon_prev)),
+        remote(E.at[288:432], E.at[720:864], sk_send.at[1], sk_recv.at[1], at(lat, lon_prev)),
+    ]
+    for copy in sk_lon:
+        copy.start()
+
+    w4x.wait_recv()
+    w4r = remote(W4.at[128:192], W4.at[192:256], w4_send.at[2], w4_recv.at[2], sibling)
+    w4r.start()
+    wr = [
+        remote(Wb.at[2, rows(j)], Wb.at[3, rows(j)], wr_send.at[j], wr_recv.at[j], sibling) for j in (0, 2, 1, 3)
+    ]
+    for arrived, onward in zip(wx, wr):
+        arrived.wait_recv()
+        onward.start()
+
     for w in range(4):
         source_row = row + (shift_lat + 6 * w)
         coarse_row = source_row >> 2
         coarse_col = source_col >> 2
         row_out = (coarse_row >= 6).astype(jnp.int32)
         col_out = (coarse_col >= 3).astype(jnp.int32)
-        cell = 48 * (col_out + 2 * row_out) + level + 6 * (coarse_row - 6 * row_out) + 2 * (coarse_col - 3 * col_out)
-        Pl[w] = onehot(jnp.where(valid, cell, -1), 192)
+        cell = 48 * col_out + row_out * (96 - 32 * col_out) + level + 6 * (coarse_row - 6 * row_out) + 2 * (coarse_col - 3 * col_out)
+        Pl[w] = onehot(jnp.where(valid, cell, -1), 128)
         label = jnp.zeros((WIN, 1), jnp.int32)
         label_t = jnp.zeros((1, WIN), jnp.int32)
         for i in range(6):
@@ -294,38 +332,9 @@
         match = jnp.where(label == label_t, 1, 0)
         bias[w] = jnp.where(seen * (match + free) > 0, 0.0, MASKED)
 
-    r = column(192)
-    out_level = (r >= 96).astype(jnp.int32)
-    frame_col = ((r - 96 * out_level) >> 3) - shift_lon
-    left = frame_col < 0
-    second = (frame_col >= 6).astype(jnp.int32)
-    place = jnp.where(left, 160 + 6 + frame_col, HALF * second + frame_col - 6 * second)
-    for b in range(3):
-        frame_row = (r & 7) + (8 * b + 6) - shift_lat
-        slot = (frame_row * 43) >> 8
-        inner = 36 * out_level + 6 * (frame_row - 6 * slot)
-        Po[b] = onehot(240 * (slot - b) + inner + place, 720)
-
-    ring(3)
-
-    sk = [
-        remote(E.at[0:144], E.at[576:720], sk_send.at[0], sk_recv.at[0], at(lat, lon_prev)),
-        remote(E.at[288:432], E.at[720:864], sk_send.at[1], sk_recv.at[1], at(lat, lon_prev)),
-        remote(Sp, E.at[864:1056], sk_send.at[2], sk_recv.at[2], at(lat_prev, lon)),
-        remote(Sp.at[0:96], E.at[1056:1152], sk_send.at[3], sk_recv.at[3], at(lat_prev, lon_prev)),
-    ]
-    for copy in sk:
-        copy.start()
-
-    w4x.wait_recv()
-    w4r = remote(W4.at[128:192], W4.at[192:256], w4_send.at[2], w4_recv.at[2], sibling)
-    w4r.start()
-    wr = [
-        remote(Wb.at[2, rows(j)], Wb.at[3, rows(j)], wr_send.at[j], wr_recv.at[j], sibling) for j in (0, 2, 1, 3)
-    ]
-    for arrived, onward in zip(wx, wr):
-        arrived.wait_recv()
-        onward.start()
+    sk_lat.wait_recv()
+    sk_both = remote(E.at[864:928], E.at[992:1056], sk_send.at[3], sk_recv.at[3], at(lat, lon_prev))
+    sk_both.start()
 
     ring(4)
 
@@ -357,6 +366,9 @@
         for w in range(2):
             PK[h, w, 0:128, :] = main[128 * w : 128 * w + 128].astype(BF)
             PK[h, w, 128:144, :] = tail[16 * w : 16 * w + 16].astype(BF)
+
+    def term(k):
+        return remote(msg.at[k], R.at[z], aa_send.at[k], aa_recv.at[z], at(lat, base + 8 * c + k))
 
     i64 = column(64)
     for w in range(2):
@@ -377,19 +389,32 @@
         tails = tails.astype(BF)
         for q in range(4):
             msg[4 * w + q, 128:144, :] = tails[16 * q : 16 * q + 16]
-
-    def term(k):
-        return remote(msg.at[k], R.at[z], aa_send.at[k], aa_recv.at[z], at(lat, base + 8 * c + k))
-
-    for k in range(8):
-
-        @pl.when(base + 8 * c + k != lon)
-        def _(k=k):
-            term(k).start()
+        for k in range(4 * w, 4 * w + 4):
+
+            @pl.when(base + 8 * c + k != lon)
+            def _(k=k):
+                term(k).start()
+
 
     @pl.when(is_home)
     def _():
         R[pl.ds(z, 1)] = msg[pl.ds(mine, 1)]
+
+    for copy in sk_lon:
+        copy.wait_recv()
+    sk_both.wait_recv()
+    for w in range(4):
+        source_row = row + (shift_lat + 6 * w)
+        cell = jnp.where(
+            source_col < 12,
+            288 * level + 24 * source_col + source_row,
+            576 + 144 * level + 24 * (source_col - 12) + source_row,
+        )
+        third = (source_col >= 6).astype(jnp.int32) + (source_col >= 12).astype(jnp.int32)
+        below = 864 + 64 * third + 10 * (source_col - 6 * third) + 5 * level + source_row - 24
+        cell = jnp.where(source_row < 24, cell, below)
+        width = 1056 if w == 3 else 864
+        skF[w] = dot(onehot(jnp.where(valid, cell, -1), width), E[0:width, :]).astype(BF)
 
     total = jnp.zeros((144, 128), F32)
     for s in range(8):
@@ -409,27 +434,12 @@
         rest = jnp.dot(pick, total[128:144], preferred_element_type=F32, precision=lax.Precision.HIGHEST)
         LE[32:48, lanes] = (cup[32:48, lanes] + rest).astype(BF)
 
-    li = [
-        remote(LE.at[0:48], LE.at[48:96], li_send.at[0], li_recv.at[0], at(lat, lon_prev)),
-        remote(LE.at[0:48], LE.at[96:144], li_send.at[1], li_recv.at[1], at(lat_prev, lon)),
-        remote(LE.at[0:48], LE.at[144:192], li_send.at[2], li_recv.at[2], at(lat_prev, lon_prev)),
-    ]
+    li_lon = remote(LE.at[0:48], LE.at[48:96], li_send.at[0], li_recv.at[0], at(lat, lon_prev))
+    li_lat = remote(LE.at[0:16], LE.at[96:112], li_send.at[1], li_recv.at[1], at(lat_prev, lon))
+    li_both = remote(LE.at[0:16], LE.at[112:128], li_send.at[2], li_recv.at[2], at(lat_prev, lon_prev))
+    li = [li_both, li_lat, li_lon]
     for copy in li:
         copy.start()
-
-    for copy in sk:
-        copy.wait_recv()
-    for w in range(4):
-        source_row = row + (shift_lat + 6 * w)
-        cell = jnp.where(
-            source_col < 12,
-            288 * level + 24 * source_col + source_row,
-            576 + 144 * level + 24 * (source_col - 12) + source_row,
-        )
-        below = 864 + 16 * source_col + 8 * level + source_row - 24
-        cell = jnp.where(source_row < 24, cell, below)
-        width = 1152 if w == 3 else 864
-        skF[w] = dot(onehot(jnp.where(valid, cell, -1), width), E[0:width, :]).astype(BF)
 
     for load in loads[4:]:
         load.wait()
@@ -460,8 +470,8 @@
 
         @pl.when(t == 0)
         def _():
-            to_lat.start()
-            to_both.start()
+            to_lat[0].start()
+            to_lat[1].start()
 
         return carry
 
@@ -470,13 +480,16 @@
             Z.at[w + 1, HALF:WIN], Z.at[w + 1, WIN : WIN + HALF], lo_send.at[w], lo_recv.at[w], at(lat, lon_next)
         )
 
-    to_lat = remote(Z.at[4, 0:WIN], Z.at[0, 0:WIN], la_send.at[0], la_recv.at[0], at(lat_next, lon))
-    to_both = remote(
-        Z.at[4, HALF:WIN], Z.at[0, WIN : WIN + HALF], la_send.at[1], la_recv.at[1], at(lat_next, lon_next)
-    )
+    to_lat = [
+        remote(Z.at[4, 80:144], Z.at[0, 80:144], la_send.at[1], la_recv.at[1], at(lat_next, lon)),
+        remote(Z.at[4, 0:64], Z.at[0, 0:64], la_send.at[0], la_recv.at[0], at(lat_next, lon)),
+    ]
+    to_both = remote(Z.at[0, 80:144], Z.at[0, 160:224], la_send.at[2], la_recv.at[2], at(lat, lon_next))
     lax.fori_loop(0, 4, window, 0)
 
-    to_lat.wait_recv()
+    to_lat[0].wait_recv()
+    to_both.start()
+    to_lat[1].wait_recv()
     to_both.wait_recv()
     for w in (3, 0, 1, 2):
         to_lon(w).wait_recv()
@@ -484,7 +497,7 @@
         taken = dot(Po[b, :, 0:240], Z[b]) + dot(Po[b, :, 240:480], Z[b + 1]) + dot(Po[b, :, 480:720], Z[b + 2])
         out[:, 8 * b : 8 * b + 8, :] = taken.astype(BF).reshape(24, 8, D1)
 
-    for copy in [*own, *wx, ws, w4x, w4s, w4r, *wr, *sk, *li, to_lat, to_both]:
+    for copy in [*own, *wx, ws, w4x, w4s, w4r, *wr, sk_lat, *sk_lon, sk_both, *li, *to_lat, to_both]:
         copy.wait_send()
 
     @pl.when(jnp.logical_not(is_home))
@@ -540,17 +553,17 @@
             pltpu.VMEM((D3, D1), BF),
             pltpu.VMEM((256, D1), BF),
             pltpu.VMEM((48, D1), F32),
-            pltpu.VMEM((192, D1), BF),
-            pltpu.VMEM((1152, D1), BF),
+            pltpu.VMEM((128, D1), BF),
+            pltpu.VMEM((1056, D1), BF),
             pltpu.VMEM((4, WIN, D1), BF),
             pltpu.VMEM((4, WIN, WIN), F32),
-            pltpu.VMEM((4, WIN, 192), BF),
+            pltpu.VMEM((4, WIN, 128), BF),
             pltpu.VMEM((3, 192, 720), BF),
             pltpu.VMEM((32, D3), BF),
             pltpu.VMEM((4, 2, 144, 192), BF),
             pltpu.VMEM((8, 144, 128), BF),
             pltpu.VMEM((8, 144, 128), BF),
-            pltpu.VMEM((192, D1), BF),
+            pltpu.VMEM((128, D1), BF),
             pltpu.VMEM((D1, 3 * D1), BF),
             pltpu.VMEM((D1, D1), BF),
             pltpu.VMEM((D1, FF), BF),
@@ -578,8 +591,8 @@
             dma((3,)),
             dma((4,)),
             dma((4,)),
-            dma((2,)),
-            dma((2,)),
+            dma((3,)),
+            dma((3,)),
         ],
         compiler_params=pltpu.CompilerParams(
             collective_id=0, has_side_effects=True, vmem_limit_bytes=56 * 1024 * 1024

time: 68.9 us -> 68.1 us (0.988)
  the two profiles are of different devices: /device:TPU:80 before, /device:TPU:30 now
where the time goes in v2:
time: 68.1 us; the launch traced here: 67.6 us
  Pallas kernels  65.7 us (96%)
  local copies, waits for them, and re-layouts  1.92 us (3%)
    pallas_call x1, Pallas kernels, local(): pl.pallas_call(kernel, out_shape=jax.ShapeDtypeStruct((24, 24, D1), BF),...  65.7 us
    unnamed x1, local copies, waits for them, and re-layouts  1.92 us

profile of v2, /device:TPU:30, one launch (start us, length us, event | category | flops | bytes accessed | tf_op | source)
XLA Modules:
  0.0 67.6 jit_solution(10259357863251837993)
XLA Ops:
  0.0 65.7 %shard_map.109 = bf16[24,24,512]{2,1,0:T(8,128)(2,1)} custom-call(s32[2]{0:T(128)} %offs.1, s32[192]{0:T(256)} %bands.1, bf16[18,2,2048]{2,1,0:T(2,128)(2,1)} %bitcast.13, bf16[576,512]{1,0:T(8,128)(2,1)} %bitcast.12, bf16[192,2048]{1,0:T(8,128)(2,1)} %bitcast.11, bf16[64,2048]{1,0:T(8,128)(2,1)} %wo.1, bf16[2048,512]{1,0:T(8,128)(2,1)} %up.1, ...), custom_call_target="tpu_custom_call" | custom-call | tf_op jit(solution)/shard_map/pallas_call | solution.py:543
  65.7 1.9 %copy.13 = bf16[2,24,12,512]{3,1,2,0:T(8,128)(2,1)} copy(bf16[2,24,12,512]{3,1,2,0:T(8,128)(2,1)} %bitcast.10) | data formatting | bytes 1179648

commit v3 on v2

--- a/solution.py
+++ b/solution.py
@@ -14,6 +14,8 @@
 HEAD = 64
 CELLS3 = 36
 OWN = 576
+PIECES = 3
+PIECE = 144 // PIECES
 SCALE = HEAD**-0.5
 EPS = 1e-05
 HALF = 80
@@ -104,6 +106,7 @@
     wfv,
     pk1,
     mix,
+    AT,
     Z,
     loc,
     own_send,
@@ -200,11 +203,22 @@
     target = z // 4
     mine = lax.rem(z, 4) * 2 + c
     is_home = target == c
+
+    def piece(t):
+        return pl.ds(PIECE * t, PIECE)
+
     own = [
-        remote(xs, G.at[mine], own_send.at[0], ring_recv.at[mine], chip(z + 1, target)),
-        remote(xs, G.at[mine], own_send.at[1], ring_recv.at[mine], chip(z - 1, target)),
+        remote(
+            xs.at[piece(t)],
+            G.at[mine, piece(t)],
+            own_send.at[2 * t + way],
+            ring_recv.at[mine, t],
+            chip(z + 1 - 2 * way, target),
+        )
+        for t in range(PIECES)
+        for way in (0, 1)
     ]
-    own_sib = remote(xs, G.at[mine], own_send.at[2], ring_recv.at[mine], sibling)
+    own_sib = remote(xs, G.at[mine], own_send.at[2 * PIECES], ring_recv.at[mine, 0], sibling)
     for copy in own:
         copy.start()
 
@@ -237,10 +251,9 @@
     def _():
         G[pl.ds(mine, 1)] = xs[...].reshape(1, 144, 512)
 
-    def relay(k, way):
-        return remote(
-            G.at[k], G.at[k], ring_send.at[k, way], ring_recv.at[k], chip(z + (1 if way == 0 else -1), c)
-        )
+    def relay(k, way, rows_, t):
+        block = G.at[k, rows_]
+        return remote(block, block, ring_send.at[k, way], ring_recv.at[k, t], chip(z + 1 - 2 * way, c))
 
     def ring_steps(s):
         for way in (0, 1):
@@ -251,14 +264,15 @@
                     yield way, lax.rem(source, 4) * 2 + core, source // 4 == c, s < limit
 
     def ring(s):
-        for way, k, here, onward in ring_steps(s):
-
-            @pl.when(here)
-            def _(way=way, k=k, onward=onward):
-                copy = relay(k, way)
-                copy.wait_recv()
-                if onward:
-                    copy.start()
+        for t in range(PIECES):
+            for way, k, here, onward in ring_steps(s):
+
+                @pl.when(here)
+                def _(way=way, k=k, onward=onward, t=t):
+                    copy = relay(k, way, piece(t), t)
+                    copy.wait_recv()
+                    if onward:
+                        copy.start()
 
     loads[3].wait()
     r128 = column(128)
@@ -336,18 +350,10 @@
     sk_both = remote(E.at[864:928], E.at[992:1056], sk_send.at[3], sk_recv.at[3], at(lat, lon_prev))
     sk_both.start()
 
-    ring(4)
-
     @pl.when(is_home)
     def _():
         k = lax.rem(z, 4) * 2 + (1 - c)
-        remote(xs, G.at[k], own_send.at[2], ring_recv.at[k], sibling).wait_recv()
-
-    for w in range(2):
-        tails = G[4 * w : 4 * w + 4, 128:144, :].reshape(64, 512)
-        for f in range(4):
-            pick = onehot((i16 >> 2) * 16 + 4 * f + (i16 & 3), 64)
-            Xt[16 * w : 16 * w + 16, 512 * f : 512 * f + 512] = dot(pick, tails).astype(BF)
+        remote(xs, G.at[k], own_send.at[0], ring_recv.at[k, 0], sibling).wait_recv()
 
     loads[2].wait()
     ws.wait_recv()
@@ -356,45 +362,44 @@
     w4s.wait_recv()
     w4r.wait_recv()
 
-    for h in range(4):
-        main = jnp.zeros((256, 192), F32)
-        for f in range(4):
-            main = main + dot_nt(
-                G[:, 32 * f : 32 * f + 32, :].reshape(256, 512), Wb[h, :, 512 * f : 512 * f + 512]
-            )
-        tail = dot_nt(Xt[...], Wb[h])
-        for w in range(2):
-            PK[h, w, 0:128, :] = main[128 * w : 128 * w + 128].astype(BF)
-            PK[h, w, 128:144, :] = tail[16 * w : 16 * w + 16].astype(BF)
-
     def term(k):
         return remote(msg.at[k], R.at[z], aa_send.at[k], aa_recv.at[z], at(lat, base + 8 * c + k))
 
     i64 = column(64)
-    for w in range(2):
+
+    def level3(w):
+        tails = G[pl.ds(4 * w, 4), 128:144, :].reshape(64, 512)
+        for f in range(4):
+            lanes = slice(512 * f, 512 * f + 512)
+            Xt[0:128, lanes] = G[pl.ds(4 * w, 4), 32 * f : 32 * f + 32, :].reshape(128, 512)
+            Xt[128:144, lanes] = dot(onehot((i16 >> 2) * 16 + 4 * f + (i16 & 3), 64), tails).astype(BF)
+        PK[...] = dot_nt(Xt[...], Wb[...].reshape(768, D3)).astype(BF)
         terms = jnp.zeros((144, 512), F32)
         for h in range(4):
-            packed = PK[h, w]
-            mixed = softmax_mix(packed[:, 0:64], packed[:, 64:128], packed[:, 128:192], None).astype(BF)
-            terms = terms + dot(mixed, W4[64 * h : 64 * h + 64, :])
+            q, k, v = (PK[:, 192 * h + 64 * i : 192 * h + 64 * i + 64] for i in range(3))
+            terms = terms + dot(softmax_mix(q, k, v, None).astype(BF), W4[64 * h : 64 * h + 64, :])
         terms = terms.astype(BF)
         tails = jnp.zeros((64, 128), F32)
         for f in range(4):
             part = terms[:, 128 * f : 128 * f + 128]
-            for q in range(4):
-                msg[4 * w + q, 32 * f : 32 * f + 32, :] = part[32 * q : 32 * q + 32]
+            msg[pl.ds(4 * w, 4), 32 * f : 32 * f + 32, :] = part[0:128].reshape(4, 32, 128)
             tails = tails + dot(
                 onehot(jnp.where(((i64 >> 2) & 3) == f, (i64 >> 4) * 4 + (i64 & 3), -1), 16), part[128:144]
             )
-        tails = tails.astype(BF)
+        msg[pl.ds(4 * w, 4), 128:144, :] = tails.astype(BF).reshape(4, 16, 128)
         for q in range(4):
-            msg[4 * w + q, 128:144, :] = tails[16 * q : 16 * q + 16]
-        for k in range(4 * w, 4 * w + 4):
+            k = 4 * w + q
 
             @pl.when(base + 8 * c + k != lon)
             def _(k=k):
                 term(k).start()
 
+    flank = lax.rem(z, 4) // 2
+    away = lax.rem(target + c, 2)
+    nearer = flank + away * (1 - 2 * flank)
+    level3(nearer)
+    ring(4)
+    level3(1 - nearer)
 
     @pl.when(is_home)
     def _():
@@ -443,37 +448,32 @@
 
     for load in loads[4:]:
         load.wait()
-    for copy in li:
-        copy.wait_recv()
-
-    def window(t, carry):
-        w = lax.rem(t + 3, 4)
-        stream = skF[w].astype(F32) + dot(Pl[w], LE[...])
+
+    def attend(w):
+        reach = 128 if w == 3 else 96
+        stream = skF[w].astype(F32) + dot(Pl[w, :, 0:reach], LE[0:reach, :])
         pk1[...] = dot(normalize(stream).astype(BF), w1v[...]).astype(BF)
         allowed = bias[w]
         for pair in range(4):
             both = []
             for h in (2 * pair, 2 * pair + 1):
-                q = pk1[:, 192 * h : 192 * h + 64]
-                k = pk1[:, 192 * h + 64 : 192 * h + 128]
-                v = pk1[:, 192 * h + 128 : 192 * h + 192]
+                q, k, v = (pk1[:, 192 * h + 64 * i : 192 * h + 64 * i + 64] for i in range(3))
                 both.append(softmax_mix(q, k, v, allowed))
             mix[:, 128 * pair : 128 * pair + 128] = jnp.concatenate(both, axis=1).astype(BF)
-        attended = stream + dot(mix[...], wo1v[...])
+        AT[w] = stream + dot(mix[...], wo1v[...])
+
+    def finish(parts):
+        attended = jnp.concatenate([AT[w, first:last, :] for w, first, last in parts], axis=0)
         normed2 = normalize(attended).astype(BF)
         result = attended
         for f in range(2):
             hidden = jax.nn.gelu(dot(normed2, wiv[:, 1024 * f : 1024 * f + 1024])).astype(BF)
             result = result + dot(hidden, wfv[1024 * f : 1024 * f + 1024, :])
-        Z[w + 1, 0:WIN, :] = result.astype(BF)
-        to_lon(w).start()
-
-        @pl.when(t == 0)
-        def _():
-            to_lat[0].start()
-            to_lat[1].start()
-
-        return carry
+        result = result.astype(BF)
+        at_row = 0
+        for w, first, last in parts:
+            Z[w + 1, first:last, :] = result[at_row : at_row + last - first]
+            at_row += last - first
 
     def to_lon(w):
         return remote(
@@ -481,23 +481,34 @@
         )
 
     to_lat = [
+        remote(Z.at[4, 80:144], Z.at[0, 160:224], la_send.at[2], la_recv.at[2], at(lat_next, lon_next)),
         remote(Z.at[4, 80:144], Z.at[0, 80:144], la_send.at[1], la_recv.at[1], at(lat_next, lon)),
         remote(Z.at[4, 0:64], Z.at[0, 0:64], la_send.at[0], la_recv.at[0], at(lat_next, lon)),
     ]
-    to_both = remote(Z.at[0, 80:144], Z.at[0, 160:224], la_send.at[2], la_recv.at[2], at(lat, lon_next))
-    lax.fori_loop(0, 4, window, 0)
-
-    to_lat[0].wait_recv()
-    to_both.start()
-    to_lat[1].wait_recv()
-    to_both.wait_recv()
+    li_lon.wait_recv()
+    attend(0)
+    li_lat.wait_recv()
+    li_both.wait_recv()
+    attend(3)
+    finish([(3, 0, WIN)])
+    for copy in to_lat:
+        copy.start()
+    to_lon(3).start()
+    attend(1)
+    attend(2)
+    finish([(w, HALF, WIN) for w in (0, 1, 2)])
+    for w in (0, 1, 2):
+        to_lon(w).start()
+    finish([(w, 0, HALF) for w in (0, 1, 2)])
+    for copy in to_lat:
+        copy.wait_recv()
     for w in (3, 0, 1, 2):
         to_lon(w).wait_recv()
     for b in range(3):
         taken = dot(Po[b, :, 0:240], Z[b]) + dot(Po[b, :, 240:480], Z[b + 1]) + dot(Po[b, :, 480:720], Z[b + 2])
         out[:, 8 * b : 8 * b + 8, :] = taken.astype(BF).reshape(24, 8, D1)
 
-    for copy in [*own, *wx, ws, w4x, w4s, w4r, *wr, sk_lat, *sk_lon, sk_both, *li, *to_lat, to_both]:
+    for copy in [*own, *wx, ws, w4x, w4s, w4r, *wr, sk_lat, *sk_lon, sk_both, *li, *to_lat]:
         copy.wait_send()
 
     @pl.when(jnp.logical_not(is_home))
@@ -510,7 +521,7 @@
 
                 @pl.when(here)
                 def _(way=way, k=k):
-                    relay(k, way).wait_send()
+                    relay(k, way, pl.ds(0, 144), 0).wait_send()
 
     for k in range(8):
 
@@ -559,8 +570,8 @@
             pltpu.VMEM((4, WIN, WIN), F32),
             pltpu.VMEM((4, WIN, 128), BF),
             pltpu.VMEM((3, 192, 720), BF),
-            pltpu.VMEM((32, D3), BF),
-            pltpu.VMEM((4, 2, 144, 192), BF),
+            pltpu.VMEM((144, D3), BF),
+            pltpu.VMEM((144, 768), BF),
             pltpu.VMEM((8, 144, 128), BF),
             pltpu.VMEM((8, 144, 128), BF),
             pltpu.VMEM((128, D1), BF),
@@ -570,11 +581,12 @@
             pltpu.VMEM((FF, D1), BF),
             pltpu.VMEM((WIN, 3 * D1), BF),
             pltpu.VMEM((WIN, D1), BF),
+            pltpu.VMEM((4, WIN, D1), F32),
             pltpu.VMEM((5, 240, D1), BF),
             dma((8,)),
-            dma((3,)),
+            dma((2 * PIECES + 1,)),
             dma((8, 2)),
-            dma((8,)),
+            dma((8, PIECES)),
             dma((4,)),
             dma((4,)),
             dma((1,)),

time: 68.1 us -> 64.6 us (0.949)
  Pallas kernels: 65.7 us -> 62.5 us
    pallas_call x1, Pallas kernels: 65.7 us -> 62.5 us  [local(): pl.pallas_call(kernel, out_shape=jax.ShapeDtypeStruct((24, 24, D1), BF),...]
where the time goes in v3:
time: 64.6 us; the launch traced here: 64.5 us
  Pallas kernels  62.5 us (97%)
  local copies, waits for them, and re-layouts  1.92 us (3%)
    pallas_call x1, Pallas kernels, local(): pl.pallas_call(kernel, out_shape=jax.ShapeDtypeStruct((24, 24, D1), BF),...  62.5 us
    unnamed x1, local copies, waits for them, and re-layouts  1.92 us

profile of v3, /device:TPU:30, one launch (start us, length us, event | category | flops | bytes accessed | tf_op | source)
XLA Modules:
  0.0 64.5 jit_solution(1355464901736388253)
XLA Ops:
  0.0 62.5 %shard_map.109 = bf16[24,24,512]{2,1,0:T(8,128)(2,1)} custom-call(s32[2]{0:T(128)} %offs.1, s32[192]{0:T(256)} %bands.1, bf16[18,2,2048]{2,1,0:T(2,128)(2,1)} %bitcast.13, bf16[576,512]{1,0:T(8,128)(2,1)} %bitcast.12, bf16[192,2048]{1,0:T(8,128)(2,1)} %bitcast.11, bf16[64,2048]{1,0:T(8,128)(2,1)} %wo.1, bf16[2048,512]{1,0:T(8,128)(2,1)} %up.1, ...), custom_call_target="tpu_custom_call" | custom-call | tf_op jit(solution)/shard_map/pallas_call | solution.py:554
  62.5 1.9 %copy.13 = bf16[2,24,12,512]{3,1,2,0:T(8,128)(2,1)} copy(bf16[2,24,12,512]{3,1,2,0:T(8,128)(2,1)} %bitcast.10) | data formatting | bytes 1179648

commit v4 on v3

--- a/solution.py
+++ b/solution.py
@@ -101,6 +101,7 @@
     R,
     LE,
     w1v,
+    w1p,
     wo1v,
     wiv,
     wfv,
@@ -287,24 +288,14 @@
 
     ring(1)
 
-    a = offs[0]
-    shift_lat = jnp.where(a >= 6, a - 6, a)
-    shift_lon = offs[1]
-    n = column(WIN)
-    valid, level, row, col = frame_cell(n)
-    valid_t, _, row_t, _ = frame_cell(lax.broadcasted_iota(jnp.int32, (1, WIN), 1))
-    source_col = col + shift_lon
-    r = column(192)
-    out_level = (r >= 96).astype(jnp.int32)
-    frame_col = ((r - 96 * out_level) >> 3) - shift_lon
-    left = frame_col < 0
-    second = (frame_col >= 6).astype(jnp.int32)
-    place = jnp.where(left, 160 + 6 + frame_col, HALF * second + frame_col - 6 * second)
-    for b in range(3):
-        frame_row = (r & 7) + (8 * b + 6) - shift_lat
-        slot = (frame_row * 43) >> 8
-        inner = 12 * (5 - (frame_row - 6 * slot)) + 6 * out_level
-        Po[b] = onehot(240 * (slot - b) + inner + place, 720)
+    loads[4].wait()
+    for pair in range(4):
+        for part in range(3):
+            first = 384 * pair + 64 * part
+            both = jnp.concatenate([w1v[:, first : first + 64], w1v[:, first + 192 : first + 256]], axis=1)
+            if part == 0:
+                both = (both.astype(F32) * SCALE).astype(BF)
+            w1p[:, 512 * part + 128 * pair : 512 * part + 128 * pair + 128] = both
 
     ring(2)
 
@@ -326,25 +317,6 @@
     for arrived, onward in zip(wx, wr):
         arrived.wait_recv()
         onward.start()
-
-    for w in range(4):
-        source_row = row + (shift_lat + 6 * w)
-        coarse_row = source_row >> 2
-        coarse_col = source_col >> 2
-        row_out = (coarse_row >= 6).astype(jnp.int32)
-        col_out = (coarse_col >= 3).astype(jnp.int32)
-        cell = 48 * col_out + row_out * (96 - 32 * col_out) + level + 6 * (coarse_row - 6 * row_out) + 2 * (coarse_col - 3 * col_out)
-        Pl[w] = onehot(jnp.where(valid, cell, -1), 128)
-        label = jnp.zeros((WIN, 1), jnp.int32)
-        label_t = jnp.zeros((1, WIN), jnp.int32)
-        for i in range(6):
-            band = bands[lax.rem(lat * 24 + shift_lat + (6 * w + i), ROWS)]
-            label = jnp.where(row == i, band, label)
-            label_t = jnp.where(row_t == i, band, label_t)
-        free = jnp.where(valid, 0, 1)
-        seen = jnp.where(valid_t, 1, 0)
-        match = jnp.where(label == label_t, 1, 0)
-        bias[w] = jnp.where(seen * (match + free) > 0, 0.0, MASKED)
 
     sk_lat.wait_recv()
     sk_both = remote(E.at[864:928], E.at[992:1056], sk_send.at[3], sk_recv.at[3], at(lat, lon_prev))
@@ -405,6 +377,44 @@
     def _():
         R[pl.ds(z, 1)] = msg[pl.ds(mine, 1)]
 
+    a = offs[0]
+    shift_lat = jnp.where(a >= 6, a - 6, a)
+    shift_lon = offs[1]
+    n = column(WIN)
+    valid, level, row, col = frame_cell(n)
+    valid_t, _, row_t, _ = frame_cell(lax.broadcasted_iota(jnp.int32, (1, WIN), 1))
+    source_col = col + shift_lon
+    for w in range(4):
+        source_row = row + (shift_lat + 6 * w)
+        coarse_row = source_row >> 2
+        coarse_col = source_col >> 2
+        row_out = (coarse_row >= 6).astype(jnp.int32)
+        col_out = (coarse_col >= 3).astype(jnp.int32)
+        cell = 48 * col_out + row_out * (96 - 32 * col_out) + level + 6 * (coarse_row - 6 * row_out) + 2 * (coarse_col - 3 * col_out)
+        Pl[w] = onehot(jnp.where(valid, cell, -1), 128)
+        label = jnp.zeros((WIN, 1), jnp.int32)
+        label_t = jnp.zeros((1, WIN), jnp.int32)
+        for i in range(6):
+            band = bands[lax.rem(lat * 24 + shift_lat + (6 * w + i), ROWS)]
+            label = jnp.where(row == i, band, label)
+            label_t = jnp.where(row_t == i, band, label_t)
+        free = jnp.where(valid, 0, 1)
+        seen = jnp.where(valid_t, 1, 0)
+        match = jnp.where(label == label_t, 1, 0)
+        bias[w] = jnp.where(seen * (match + free) > 0, 0.0, MASKED)
+
+    r = column(192)
+    out_level = (r >= 96).astype(jnp.int32)
+    frame_col = ((r - 96 * out_level) >> 3) - shift_lon
+    left = frame_col < 0
+    second = (frame_col >= 6).astype(jnp.int32)
+    place = jnp.where(left, 160 + 6 + frame_col, HALF * second + frame_col - 6 * second)
+    for b in range(3):
+        frame_row = (r & 7) + (8 * b + 6) - shift_lat
+        slot = (frame_row * 43) >> 8
+        inner = 12 * (5 - (frame_row - 6 * slot)) + 6 * out_level
+        Po[b] = onehot(240 * (slot - b) + inner + place, 720)
+
     for copy in sk_lon:
         copy.wait_recv()
     sk_both.wait_recv()
@@ -446,20 +456,30 @@
     for copy in li:
         copy.start()
 
-    for load in loads[4:]:
+    for load in loads[5:]:
         load.wait()
+
+    low = lax.broadcasted_iota(jnp.int32, (WIN, 128), 1) < HEAD
+    zero = jnp.zeros((WIN, 128), BF)
+    one = jnp.ones((WIN, 128), BF)
 
     def attend(w):
         reach = 128 if w == 3 else 96
         stream = skF[w].astype(F32) + dot(Pl[w, :, 0:reach], LE[0:reach, :])
-        pk1[...] = dot(normalize(stream).astype(BF), w1v[...]).astype(BF)
+        pk1[...] = dot(normalize(stream).astype(BF), w1p[...]).astype(BF)
         allowed = bias[w]
         for pair in range(4):
-            both = []
-            for h in (2 * pair, 2 * pair + 1):
-                q, k, v = (pk1[:, 192 * h + 64 * i : 192 * h + 64 * i + 64] for i in range(3))
-                both.append(softmax_mix(q, k, v, allowed))
-            mix[:, 128 * pair : 128 * pair + 128] = jnp.concatenate(both, axis=1).astype(BF)
+            lanes = slice(128 * pair, 128 * pair + 128)
+            q, k, v = (pk1[:, 512 * i + 128 * pair : 512 * i + 128 * pair + 128] for i in range(3))
+            sums = []
+            for first in (True, False):
+                here = low if first else jnp.logical_not(low)
+                scores = dot_nt(jnp.where(here, q, zero), k) + allowed
+                weights = jnp.exp(scores - jnp.max(scores, axis=1, keepdims=True)).astype(BF)
+                sums.append(dot(weights, jnp.where(here, v, one)))
+            mixed = jnp.where(low, sums[0], sums[1])
+            total = pltpu.roll(jnp.where(low, sums[1], sums[0]), 64, 1)
+            mix[:, lanes] = (mixed * (1.0 / total)).astype(BF)
         AT[w] = stream + dot(mix[...], wo1v[...])
 
     def finish(parts):
@@ -490,15 +510,16 @@
     li_lat.wait_recv()
     li_both.wait_recv()
     attend(3)
-    finish([(3, 0, WIN)])
+    finish([(3, 0, WIN), (0, HALF, WIN)])
     for copy in to_lat:
         copy.start()
     to_lon(3).start()
+    to_lon(0).start()
     attend(1)
     attend(2)
-    finish([(w, HALF, WIN) for w in (0, 1, 2)])
-    for w in (0, 1, 2):
-        to_lon(w).start()
+    finish([(1, HALF, WIN), (2, HALF, WIN)])
+    to_lon(1).start()
+    to_lon(2).start()
     finish([(w, 0, HALF) for w in (0, 1, 2)])
     for copy in to_lat:
         copy.wait_recv()
@@ -576,6 +597,7 @@
             pltpu.VMEM((8, 144, 128), BF),
             pltpu.VMEM((128, D1), BF),
             pltpu.VMEM((D1, 3 * D1), BF),
+            pltpu.VMEM((D1, 3 * D1), BF),
             pltpu.VMEM((D1, D1), BF),
             pltpu.VMEM((D1, FF), BF),
             pltpu.VMEM((FF, D1), BF),

time: 64.6 us -> 61.1 us (0.946)
  Pallas kernels: 62.5 us -> 59.1 us
    pallas_call x1, Pallas kernels: 62.5 us -> 59.1 us  [local(): pl.pallas_call(kernel, out_shape=jax.ShapeDtypeStruct((24, 24, D1), BF),...]
where the time goes in v4:
time: 61.1 us; the launch traced here: 61 us
  Pallas kernels  59.1 us (97%)
  local copies, waits for them, and re-layouts  1.92 us (3%)
    pallas_call x1, Pallas kernels, local(): pl.pallas_call(kernel, out_shape=jax.ShapeDtypeStruct((24, 24, D1), BF),...  59.1 us
    unnamed x1, local copies, waits for them, and re-layouts  1.92 us

profile of v4, /device:TPU:30, one launch (start us, length us, event | category | flops | bytes accessed | tf_op | source)
XLA Modules:
  0.0 61.0 jit_solution(2809999856410029561)
XLA Ops:
  0.0 59.1 %shard_map.109 = bf16[24,24,512]{2,1,0:T(8,128)(2,1)} custom-call(s32[2]{0:T(128)} %offs.1, s32[192]{0:T(256)} %bands.1, bf16[18,2,2048]{2,1,0:T(2,128)(2,1)} %bitcast.13, bf16[576,512]{1,0:T(8,128)(2,1)} %bitcast.12, bf16[192,2048]{1,0:T(8,128)(2,1)} %bitcast.11, bf16[64,2048]{1,0:T(8,128)(2,1)} %wo.1, bf16[2048,512]{1,0:T(8,128)(2,1)} %up.1, ...), custom_call_target="tpu_custom_call" | custom-call | tf_op jit(solution)/shard_map/pallas_call | solution.py:575
  59.1 1.9 %copy.13 = bf16[2,24,12,512]{3,1,2,0:T(8,128)(2,1)} copy(bf16[2,24,12,512]{3,1,2,0:T(8,128)(2,1)} %bitcast.10) | data formatting | bytes 1179648

commit v5 on v4

--- a/solution.py
+++ b/solution.py
@@ -60,13 +60,17 @@
     return valid, sixth & 1, 5 - (sixth >> 1), m - 6 * sixth + 6 * half
 
 
-def softmax_mix(q, k, v, bias):
-    scores = dot_nt(q, k) * SCALE
-    if bias is not None:
-        scores = scores + bias
-    weights = jnp.exp(scores - jnp.max(scores, axis=1, keepdims=True))
-    total = jnp.sum(weights, axis=1, keepdims=True)
-    return dot(weights.astype(BF), v) * (1.0 / total)
+def pair_mix(q, k, v, allowed):
+    low = lax.broadcasted_iota(jnp.int32, q.shape, 1) < HEAD
+    sums = []
+    for here in (low, jnp.logical_not(low)):
+        scores = dot_nt(jnp.where(here, q, jnp.zeros_like(q)), k)
+        if allowed is not None:
+            scores = scores + allowed
+        weights = jnp.exp(scores - jnp.max(scores, axis=1, keepdims=True)).astype(BF)
+        sums.append(dot(weights, jnp.where(here, v, jnp.ones_like(v))))
+    total = pltpu.roll(jnp.where(low, sums[1], sums[0]), HEAD, 1)
+    return jnp.where(low, sums[0], sums[1]) * (1.0 / total)
 
 
 def kernel(
@@ -94,7 +98,10 @@
     skF,
     bias,
     Pl,
-    Po,
+    PA,
+    PB,
+    PC,
+    OA,
     Xt,
     PK,
     msg,
@@ -109,6 +116,7 @@
     mix,
     AT,
     Z,
+    ZB,
     loc,
     own_send,
     ring_send,
@@ -162,7 +170,7 @@
     loads = [
         pltpu.make_async_copy(src, dst, loc.at[i])
         for i, (src, dst) in enumerate(
-            [(up, upv), (wo, wov), (wq, Wb.at[0]), (skip, E.at[0:OWN]), (w1, w1v), (wo1, wo1v), (wi, wiv), (wf, wfv)]
+            [(up, upv), (wo, wov), (wq, Wb.at[:, 0]), (skip, E.at[0:OWN]), (w1, w1v), (wo1, wo1v), (wi, wiv), (wf, wfv)]
         )
     ]
     for load in loads:
@@ -196,8 +204,9 @@
         rest = rest + dot(pick, part[32:48])
     xs[128:144, :] = rest.astype(BF)
 
-    for first in (64, 144, 224):
+    for first in (64, 144):
         Z[0, first : first + 16, :] = jnp.zeros((16, D1), BF)
+    ZB[0, 64:80, :] = jnp.zeros((16, D1), BF)
 
     pl.semaphore_wait(barrier, len(greeted))
 
@@ -228,15 +237,15 @@
         own_sib.start()
 
     def rows(j):
-        return pl.ds(48 * j, 48)
+        return pl.ds(16 * j, 16)
 
     wx = [
-        remote(wq.at[rows(j)], Wb.at[2, rows(j)], wx_send.at[j], wx_recv.at[j], near if j < 2 else far)
+        remote(wq.at[:, rows(j)], Wb.at[:, 2, rows(j)], wx_send.at[j], wx_recv.at[j], near if j < 2 else far)
         for j in (0, 2, 1, 3)
     ]
     for copy in wx:
         copy.start()
-    ws = remote(wq, Wb.at[1], ws_send.at[0], ws_recv.at[0], sibling)
+    ws = remote(wq, Wb.at[:, 1], ws_send.at[0], ws_recv.at[0], sibling)
     ws.start()
 
     loads[0].wait()
@@ -288,6 +297,17 @@
 
     ring(1)
 
+    ring(2)
+
+    ring(3)
+
+    sk_lon = [
+        remote(E.at[0:144], E.at[576:720], sk_send.at[0], sk_recv.at[0], at(lat, lon_prev)),
+        remote(E.at[288:432], E.at[720:864], sk_send.at[1], sk_recv.at[1], at(lat, lon_prev)),
+    ]
+    for copy in sk_lon:
+        copy.start()
+
     loads[4].wait()
     for pair in range(4):
         for part in range(3):
@@ -297,22 +317,11 @@
                 both = (both.astype(F32) * SCALE).astype(BF)
             w1p[:, 512 * part + 128 * pair : 512 * part + 128 * pair + 128] = both
 
-    ring(2)
-
-    ring(3)
-
-    sk_lon = [
-        remote(E.at[0:144], E.at[576:720], sk_send.at[0], sk_recv.at[0], at(lat, lon_prev)),
-        remote(E.at[288:432], E.at[720:864], sk_send.at[1], sk_recv.at[1], at(lat, lon_prev)),
-    ]
-    for copy in sk_lon:
-        copy.start()
-
     w4x.wait_recv()
     w4r = remote(W4.at[128:192], W4.at[192:256], w4_send.at[2], w4_recv.at[2], sibling)
     w4r.start()
     wr = [
-        remote(Wb.at[2, rows(j)], Wb.at[3, rows(j)], wr_send.at[j], wr_recv.at[j], sibling) for j in (0, 2, 1, 3)
+        remote(Wb.at[:, 2, rows(j)], Wb.at[:, 3, rows(j)], wr_send.at[j], wr_recv.at[j], sibling) for j in (0, 2, 1, 3)
     ]
     for arrived, onward in zip(wx, wr):
         arrived.wait_recv()
@@ -345,11 +354,13 @@
             lanes = slice(512 * f, 512 * f + 512)
             Xt[0:128, lanes] = G[pl.ds(4 * w, 4), 32 * f : 32 * f + 32, :].reshape(128, 512)
             Xt[128:144, lanes] = dot(onehot((i16 >> 2) * 16 + 4 * f + (i16 & 3), 64), tails).astype(BF)
-        PK[...] = dot_nt(Xt[...], Wb[...].reshape(768, D3)).astype(BF)
+        packed = dot_nt(Xt[...], Wb[...].reshape(768, D3))
+        PK[:, 0:256] = (packed[:, 0:256] * SCALE).astype(BF)
+        PK[:, 256:768] = packed[:, 256:768].astype(BF)
         terms = jnp.zeros((144, 512), F32)
-        for h in range(4):
-            q, k, v = (PK[:, 192 * h + 64 * i : 192 * h + 64 * i + 64] for i in range(3))
-            terms = terms + dot(softmax_mix(q, k, v, None).astype(BF), W4[64 * h : 64 * h + 64, :])
+        for pair in range(2):
+            q, k, v = (PK[:, 256 * i + 128 * pair : 256 * i + 128 * pair + 128] for i in range(3))
+            terms = terms + dot(pair_mix(q, k, v, None).astype(BF), W4[128 * pair : 128 * pair + 128, :])
         terms = terms.astype(BF)
         tails = jnp.zeros((64, 128), F32)
         for f in range(4):
@@ -408,12 +419,15 @@
     frame_col = ((r - 96 * out_level) >> 3) - shift_lon
     left = frame_col < 0
     second = (frame_col >= 6).astype(jnp.int32)
-    place = jnp.where(left, 160 + 6 + frame_col, HALF * second + frame_col - 6 * second)
     for b in range(3):
         frame_row = (r & 7) + (8 * b + 6) - shift_lat
         slot = (frame_row * 43) >> 8
-        inner = 12 * (5 - (frame_row - 6 * slot)) + 6 * out_level
-        Po[b] = onehot(240 * (slot - b) + inner + place, 720)
+        inner = 12 * (5 - (frame_row - 6 * slot)) + 6 * out_level + frame_col
+        kept = WIN * (slot - max(b, 1)) + (HALF - 6) * second + inner
+        PA[b] = onehot(jnp.where(left, -1, kept), 3 * WIN)
+        PB[b] = onehot(jnp.where(left, HALF * (slot - b) + inner + 6, -1), 3 * HALF)
+        if b == 0:
+            PC[...] = onehot(jnp.where(left | (slot > 0), -1, kept + WIN), WIN)
 
     for copy in sk_lon:
         copy.wait_recv()
@@ -443,10 +457,7 @@
     for f in range(4):
         lanes = slice(128 * f, 128 * f + 128)
         LE[0:32, lanes] = (cup[0:32, lanes] + total[32 * f : 32 * f + 32]).astype(BF)
-        pick = jnp.where(
-            (lax.broadcasted_iota(jnp.int32, (16, 16), 1) == 4 * f + i16) & (i16 < 4), 1.0, 0.0
-        )
-        rest = jnp.dot(pick, total[128:144], preferred_element_type=F32, precision=lax.Precision.HIGHEST)
+        rest = jnp.concatenate([total[128 + 4 * f : 132 + 4 * f], jnp.zeros((12, 128), F32)], axis=0)
         LE[32:48, lanes] = (cup[32:48, lanes] + rest).astype(BF)
 
     li_lon = remote(LE.at[0:48], LE.at[48:96], li_send.at[0], li_recv.at[0], at(lat, lon_prev))
@@ -459,28 +470,24 @@
     for load in loads[5:]:
         load.wait()
 
-    low = lax.broadcasted_iota(jnp.int32, (WIN, 128), 1) < HEAD
-    zero = jnp.zeros((WIN, 128), BF)
-    one = jnp.ones((WIN, 128), BF)
+    def project(parts, reach):
+        chosen = jnp.concatenate([Pl[w, first:last, 0:reach] for w, first, last in parts], axis=0)
+        taken = jnp.concatenate([skF[w, first:last, :] for w, first, last in parts], axis=0)
+        stream = taken.astype(F32) + dot(chosen, LE[0:reach, :])
+        packed = dot(normalize(stream).astype(BF), w1p[...]).astype(BF)
+        at_row = 0
+        for w, first, last in parts:
+            here = slice(at_row, at_row + last - first)
+            AT[w, first:last, :] = stream[here]
+            pk1[w, first:last, :] = packed[here]
+            at_row += last - first
 
     def attend(w):
-        reach = 128 if w == 3 else 96
-        stream = skF[w].astype(F32) + dot(Pl[w, :, 0:reach], LE[0:reach, :])
-        pk1[...] = dot(normalize(stream).astype(BF), w1p[...]).astype(BF)
-        allowed = bias[w]
         for pair in range(4):
             lanes = slice(128 * pair, 128 * pair + 128)
-            q, k, v = (pk1[:, 512 * i + 128 * pair : 512 * i + 128 * pair + 128] for i in range(3))
-            sums = []
-            for first in (True, False):
-                here = low if first else jnp.logical_not(low)
-                scores = dot_nt(jnp.where(here, q, zero), k) + allowed
-                weights = jnp.exp(scores - jnp.max(scores, axis=1, keepdims=True)).astype(BF)
-                sums.append(dot(weights, jnp.where(here, v, one)))
-            mixed = jnp.where(low, sums[0], sums[1])
-            total = pltpu.roll(jnp.where(low, sums[1], sums[0]), 64, 1)
-            mix[:, lanes] = (mixed * (1.0 / total)).astype(BF)
-        AT[w] = stream + dot(mix[...], wo1v[...])
+            q, k, v = (pk1[w, :, 512 * i + 128 * pair : 512 * i + 128 * pair + 128] for i in range(3))
+            mix[:, lanes] = pair_mix(q, k, v, bias[w]).astype(BF)
+        AT[w] = AT[w] + dot(mix[...], wo1v[...])
 
     def finish(parts):
         attended = jnp.concatenate([AT[w, first:last, :] for w, first, last in parts], axis=0)
@@ -497,18 +504,21 @@
 
     def to_lon(w):
         return remote(
-            Z.at[w + 1, HALF:WIN], Z.at[w + 1, WIN : WIN + HALF], lo_send.at[w], lo_recv.at[w], at(lat, lon_next)
+            Z.at[w + 1, HALF:WIN], ZB.at[w + 1], lo_send.at[w], lo_recv.at[w], at(lat, lon_next)
         )
 
     to_lat = [
-        remote(Z.at[4, 80:144], Z.at[0, 160:224], la_send.at[2], la_recv.at[2], at(lat_next, lon_next)),
+        remote(Z.at[4, 80:144], ZB.at[0, 0:64], la_send.at[2], la_recv.at[2], at(lat_next, lon_next)),
         remote(Z.at[4, 80:144], Z.at[0, 80:144], la_send.at[1], la_recv.at[1], at(lat_next, lon)),
         remote(Z.at[4, 0:64], Z.at[0, 0:64], la_send.at[0], la_recv.at[0], at(lat_next, lon)),
     ]
+    project([(w, 0, HALF) for w in (0, 1, 2)], 48)
     li_lon.wait_recv()
+    project([(w, HALF, WIN) for w in (0, 1, 2)], 96)
     attend(0)
     li_lat.wait_recv()
     li_both.wait_recv()
+    project([(3, 0, WIN)], 128)
     attend(3)
     finish([(3, 0, WIN), (0, HALF, WIN)])
     for copy in to_lat:
@@ -521,13 +531,18 @@
     to_lon(1).start()
     to_lon(2).start()
     finish([(w, 0, HALF) for w in (0, 1, 2)])
+    OA[0] = dot(PA[0, :, 0 : 2 * WIN], Z[1:3].reshape(2 * WIN, D1)).astype(BF)
+    for b in (1, 2):
+        OA[b] = dot(PA[b], Z[b : b + 3].reshape(3 * WIN, D1)).astype(BF)
     for copy in to_lat:
         copy.wait_recv()
     for w in (3, 0, 1, 2):
         to_lon(w).wait_recv()
     for b in range(3):
-        taken = dot(Po[b, :, 0:240], Z[b]) + dot(Po[b, :, 240:480], Z[b + 1]) + dot(Po[b, :, 480:720], Z[b + 2])
-        out[:, 8 * b : 8 * b + 8, :] = taken.astype(BF).reshape(24, 8, D1)
+        back = dot(PB[b], ZB[b : b + 3].reshape(3 * HALF, D1))
+        if b == 0:
+            back = back + dot(PC[...], Z[0])
+        out[:, 8 * b : 8 * b + 8, :] = (OA[b].astype(F32) + back).astype(BF).reshape(24, 8, D1)
 
     for copy in [*own, *wx, ws, w4x, w4s, w4r, *wr, sk_lat, *sk_lon, sk_both, *li, *to_lat]:
         copy.wait_send()
@@ -580,7 +595,7 @@
         scratch_shapes=[
             pltpu.VMEM((144, 512), BF),
             pltpu.VMEM((8, 144, 512), BF),
-            pltpu.VMEM((4, 192, D3), BF),
+            pltpu.VMEM((3, 4, HEAD, D3), BF),
             pltpu.VMEM((64, D3), BF),
             pltpu.VMEM((D3, D1), BF),
             pltpu.VMEM((256, D1), BF),
@@ -590,7 +605,10 @@
             pltpu.VMEM((4, WIN, D1), BF),
             pltpu.VMEM((4, WIN, WIN), F32),
             pltpu.VMEM((4, WIN, 128), BF),
-            pltpu.VMEM((3, 192, 720), BF),
+            pltpu.VMEM((3, 192, 3 * WIN), BF),
+            pltpu.VMEM((3, 192, 3 * HALF), BF),
+            pltpu.VMEM((192, WIN), BF),
+            pltpu.VMEM((3, 192, D1), BF),
             pltpu.VMEM((144, D3), BF),
             pltpu.VMEM((144, 768), BF),
             pltpu.VMEM((8, 144, 128), BF),
@@ -601,10 +619,11 @@
             pltpu.VMEM((D1, D1), BF),
             pltpu.VMEM((D1, FF), BF),
             pltpu.VMEM((FF, D1), BF),
-            pltpu.VMEM((WIN, 3 * D1), BF),
+            pltpu.VMEM((4, WIN, 3 * D1), BF),
             pltpu.VMEM((WIN, D1), BF),
             pltpu.VMEM((4, WIN, D1), F32),
-            pltpu.VMEM((5, 240, D1), BF),
+            pltpu.VMEM((5, WIN, D1), BF),
+            pltpu.VMEM((5, HALF, D1), BF),
             dma((8,)),
             dma((2 * PIECES + 1,)),
             dma((8, 2)),
@@ -636,7 +655,7 @@
         bands,
         cells,
         jnp.transpose(skip, (0, 2, 1, 3)).reshape(OWN, D1),
-        qkv3_weight.T,
+        qkv3_weight.T.reshape(3, HEAD, D3),
         out3_weight,
         up_weight,
         qkv1_weight,

time: 61.1 us -> 60.5 us (level)
  the two profiles are of different devices: /device:TPU:30 before, /device:TPU:24 now
where the time goes in v5:
time: 60.5 us; the launch traced here: 60.4 us
  Pallas kernels  58.4 us (97%)
  local copies, waits for them, and re-layouts  1.92 us (3%)
    pallas_call x1, Pallas kernels, local(): pl.pallas_call(kernel, out_shape=jax.ShapeDtypeStruct((24, 24, D1), BF),...  58.4 us
    unnamed x1, local copies, waits for them, and re-layouts  1.92 us

profile of v5, /device:TPU:24, one launch (start us, length us, event | category | flops | bytes accessed | tf_op | source)
XLA Modules:
  0.0 60.4 jit_solution(13045230412805881255)
XLA Ops:
  0.0 58.4 %shard_map.109 = bf16[24,24,512]{2,1,0:T(8,128)(2,1)} custom-call(s32[2]{0:T(128)} %offs.1, s32[192]{0:T(256)} %bands.1, bf16[18,2,2048]{2,1,0:T(2,128)(2,1)} %bitcast.15, bf16[576,512]{1,0:T(8,128)(2,1)} %bitcast.14, bf16[3,64,2048]{2,1,0:T(8,128)(2,1)} %bitcast.13, bf16[64,2048]{1,0:T(8,128)(2,1)} %wo.1, bf16[2048,512]{1,0:T(8,128)(2,1)} %up.1, ...), custom_call_target="tpu_custom_call" | custom-call | tf_op jit(solution)/shard_map/pallas_call | solution.py:590
  58.5 1.9 %copy.13 = bf16[2,24,12,512]{3,1,2,0:T(8,128)(2,1)} copy(bf16[2,24,12,512]{3,1,2,0:T(8,128)(2,1)} %bitcast.12) | data formatting | bytes 1179648

commit v6 on v5

--- a/solution.py
+++ b/solution.py
@@ -414,21 +414,6 @@
         match = jnp.where(label == label_t, 1, 0)
         bias[w] = jnp.where(seen * (match + free) > 0, 0.0, MASKED)
 
-    r = column(192)
-    out_level = (r >= 96).astype(jnp.int32)
-    frame_col = ((r - 96 * out_level) >> 3) - shift_lon
-    left = frame_col < 0
-    second = (frame_col >= 6).astype(jnp.int32)
-    for b in range(3):
-        frame_row = (r & 7) + (8 * b + 6) - shift_lat
-        slot = (frame_row * 43) >> 8
-        inner = 12 * (5 - (frame_row - 6 * slot)) + 6 * out_level + frame_col
-        kept = WIN * (slot - max(b, 1)) + (HALF - 6) * second + inner
-        PA[b] = onehot(jnp.where(left, -1, kept), 3 * WIN)
-        PB[b] = onehot(jnp.where(left, HALF * (slot - b) + inner + 6, -1), 3 * HALF)
-        if b == 0:
-            PC[...] = onehot(jnp.where(left | (slot > 0), -1, kept + WIN), WIN)
-
     for copy in sk_lon:
         copy.wait_recv()
     sk_both.wait_recv()
@@ -515,22 +500,39 @@
     project([(w, 0, HALF) for w in (0, 1, 2)], 48)
     li_lon.wait_recv()
     project([(w, HALF, WIN) for w in (0, 1, 2)], 96)
-    attend(0)
     li_lat.wait_recv()
     li_both.wait_recv()
     project([(3, 0, WIN)], 128)
     attend(3)
-    finish([(3, 0, WIN), (0, HALF, WIN)])
+    finish([(3, 0, WIN)])
     for copy in to_lat:
         copy.start()
     to_lon(3).start()
+    attend(0)
+    attend(1)
+    finish([(0, HALF, WIN), (1, HALF, WIN)])
     to_lon(0).start()
-    attend(1)
+    to_lon(1).start()
     attend(2)
-    finish([(1, HALF, WIN), (2, HALF, WIN)])
-    to_lon(1).start()
+    finish([(2, HALF, WIN)])
     to_lon(2).start()
     finish([(w, 0, HALF) for w in (0, 1, 2)])
+
+    r = column(192)
+    out_level = (r >= 96).astype(jnp.int32)
+    frame_col = ((r - 96 * out_level) >> 3) - shift_lon
+    left = frame_col < 0
+    second = (frame_col >= 6).astype(jnp.int32)
+    for b in range(3):
+        frame_row = (r & 7) + (8 * b + 6) - shift_lat
+        slot = (frame_row * 43) >> 8
+        inner = 12 * (5 - (frame_row - 6 * slot)) + 6 * out_level + frame_col
+        kept = WIN * (slot - max(b, 1)) + (HALF - 6) * second + inner
+        PA[b] = onehot(jnp.where(left, -1, kept), 3 * WIN)
+        PB[b] = onehot(jnp.where(left, HALF * (slot - b) + inner + 6, -1), 3 * HALF)
+        if b == 0:
+            PC[...] = onehot(jnp.where(left | (slot > 0), -1, kept + WIN), WIN)
+
     OA[0] = dot(PA[0, :, 0 : 2 * WIN], Z[1:3].reshape(2 * WIN, D1)).astype(BF)
     for b in (1, 2):
         OA[b] = dot(PA[b], Z[b : b + 3].reshape(3 * WIN, D1)).astype(BF)

time: 60.5 us -> 60 us (level)
  the two profiles are of different devices: /device:TPU:24 before, /device:TPU:30 now
where the time goes in v6:
time: 60 us; the launch traced here: 58.9 us
  Pallas kernels  56.9 us (95%)
  local copies, waits for them, and re-layouts  1.92 us (3%)
    pallas_call x1, Pallas kernels, local(): pl.pallas_call(kernel, out_shape=jax.ShapeDtypeStruct((24, 24, D1), BF),...  56.9 us
    unnamed x1, local copies, waits for them, and re-layouts  1.92 us

profile of v6, /device:TPU:30, one launch (start us, length us, event | category | flops | bytes accessed | tf_op | source)
XLA Modules:
  0.0 58.9 jit_solution(16593537911384523831)
XLA Ops:
  0.0 56.9 %shard_map.109 = bf16[24,24,512]{2,1,0:T(8,128)(2,1)} custom-call(s32[2]{0:T(128)} %offs.1, s32[192]{0:T(256)} %bands.1, bf16[18,2,2048]{2,1,0:T(2,128)(2,1)} %bitcast.15, bf16[576,512]{1,0:T(8,128)(2,1)} %bitcast.14, bf16[3,64,2048]{2,1,0:T(8,128)(2,1)} %bitcast.13, bf16[64,2048]{1,0:T(8,128)(2,1)} %wo.1, bf16[2048,512]{1,0:T(8,128)(2,1)} %up.1, ...), custom_call_target="tpu_custom_call" | custom-call | tf_op jit(solution)/shard_map/pallas_call | solution.py:592
  56.9 1.9 %copy.13 = bf16[2,24,12,512]{3,1,2,0:T(8,128)(2,1)} copy(bf16[2,24,12,512]{3,1,2,0:T(8,128)(2,1)} %bitcast.12) | data formatting | bytes 1179648
